TPU v7x, 512 devices: a whole 4x4x16 slice. The times are simulated.
512 devices in a mesh: gx: 16 (over z_lo, x), gy: 4 (over y), gz: 8 (over z_hi, core).
Axes of the slice: x: 4, y: 4, z: 16 (z_hi: 4, z_lo: 4; z = z_hi * 4 + z_lo), core: 2. Of those that a mesh axis runs over, the one named last changes fastest.
Arguments:
- tensor: float32 [32, 512, 32, 512], P(None, 'gx', 'gz', 'gy'), may hold values from -11 to 11, as said below
- factor: float32 [512, 64], P('gx'), may hold values from -0.25 to 0.25
Outputs:
- core_tensor: float32 [32, 64, 32, 512], P('gx', None, 'gz', 'gy')
- gram_matrix: float32 [512, 512], P('gy')
Inputs may be any that keep to these rules, and one draw needn't show every extreme that they name: `tensor`: real-valued field, rough from cell to cell.
All inputs are finite; a program needn't handle non-finite values.
Results may differ from a plain program's by a relative error of at most 0.00012.
Values sent between devices are 32-bit elements; how exact they have to be, the bound alone decides.
No kernel may reach another device: no remote copies, remote signals or barrier semaphores. Data moves between devices by JAX's collectives and lax.ppermute only.
A program may use at most 64 MiB of HBM per device.

v0:
```python
import jax
import jax.numpy as jnp
from jax import lax
from jax.sharding import PartitionSpec as P


def local(tensor, factor):
    var_count = tensor.shape[0]
    rank_count = factor.shape[1]
    core_tensor = lax.psum_scatter(
        jnp.einsum("ir,vikj->vrkj", factor, tensor, precision=lax.Precision.HIGHEST),
        "gx",
        scatter_dimension=0,
        tiled=True,
    )
    inverse_count = 1.0 / float(var_count * rank_count * tensor.shape[2] * lax.axis_size("gz"))
    gram_rows = jnp.einsum(
        "vrkj,vrkl->jl",
        core_tensor,
        lax.all_gather(core_tensor, "gy", axis=3, tiled=True),
        precision=lax.Precision.HIGHEST,
    )
    gram_matrix = lax.psum(gram_rows * inverse_count, ("gx", "gz"))
    return (core_tensor, gram_matrix)


def solution(mesh):
    in_specs = (P(None, "gx", "gz", "gy"), P("gx", None))
    out_specs = (P("gx", None, "gz", "gy"), P("gy", None))
    return jax.shard_map(local, mesh=mesh, in_specs=in_specs, out_specs=out_specs, check_vma=False)
```

profile of v0, /device:TPU:1, one launch (start us, length us, event | category | flops | bytes accessed | tf_op | source)
XLA Modules:
  0.0 492.3 jit_solution(15267389651214590650)
XLA Ops:
  7.2 0.0 copy-start
  7.2 0.0 reduce-scatter.2.cloned.1.call-start
  7.2 0.7 copy-done
  7.9 7.0 %convolution_bitcast_fusion = f32[32,64,4,128]{3,1,2,0:T(8,128)} fusion(f32[32,32,4,128]{3,2,1,0:T(4,128)} %param.2, f32[32,64]{1,0:T(8,128)S(1)} %copy-done), kind=kOutput, calls=%fused_computation | convolution fusion | flops 402653184 | bytes 6299648 | tf_op jit(solution)/shard_map/ir,vikj->vrkj/dot_general | solution.py:11
  14.9 0.0 reduce-scatter.2.cloned.1.call-update
  14.9 0.0 all-gather.2.cloned.1.call-start
  15.0 94.2 %reduce-scatter.2.cloned.1.call-done = f32[2,64,4,128]{3,1,2,0:T(8,128)} async-done(((f32[32,64,4,128]{3,1,2,0:T(8,128)}), f32[2,64,4,128]{3,1,2,0:T(8,128)}) %reduce-scatter.2.cloned.1.call-update) | async-done | bytes 262160 | tf_op jit(solution)/shard_map/reduce_scatter | solution.py:10
  109.2 0.0 copy-start.1
  109.2 0.0 all-gather.2.cloned.1.call-update
  109.2 0.0 all-reduce.2.cloned.1.call-start
  109.2 41.3 %all-gather.2.cloned.1.call-done = f32[2,64,4,512]{3,1,2,0:T(8,128)} async-done(((f32[2,64,4,128]{3,1,2,0:T(8,128)}), f32[2,64,4,512]{3,1,2,0:T(8,128)}) %all-gather.2.cloned.1.call-update) | async-done | bytes 1048592 | tf_op jit(solution)/shard_map/all_gather | solution.py:20
  150.6 2.8 fusion.1
  153.4 0.0 all-reduce.2.cloned.1.call-update
  153.4 0.0 copy-done.1
  153.4 0.9 copy.7
  154.3 329.8 %all-reduce.2.cloned.1.call-done = f32[128,512]{1,0:T(8,128)} async-done(((f32[128,512]{1,0:T(8,128)}), f32[128,512]{1,0:T(8,128)}) %all-reduce.2.cloned.1.call-update) | async-done | bytes 262160 | tf_op jit(solution)/shard_map/psum | solution.py:23
  484.1 1.7 copy.17
Async XLA Ops:
  7.2 0.7 copy-start
  7.2 102.0 %reduce-scatter.2.cloned.1.call-start = ((), (), s32[]{:S(2)}) async-start(), calls=%async_computation.1 | async-start | bytes 4456448 | tf_op jit(solution)/shard_map/reduce_scatter | solution.py:10
  14.9 135.7 %all-gather.2.cloned.1.call-start = ((), (), s32[]{:S(2)}) async-start(), calls=%async_computation.2 | async-start | bytes 1310720 | tf_op jit(solution)/shard_map/all_gather | solution.py:20
  109.2 44.2 %copy-start.1 = (f32[2,64,4,128]{3,1,2,0:T(8,128)S(1)}, f32[2,64,4,128]{3,1,2,0:T(8,128)}, u32[]{:S(2)}) copy-start(f32[2,64,4,128]{3,1,2,0:T(8,128)} %reduce-scatter.2.cloned.1.call-done) | copy-start | bytes 786436
  109.2 374.9 %all-reduce.2.cloned.1.call-start = ((), (), s32[]{:S(2)}) async-start(), calls=%async_computation.3 | async-start | bytes 524288 | tf_op jit(solution)/shard_map/psum | solution.py:23
Sparse Core Ops, SparseCore 0:
  15.0 94.0 reduce-scatter.1
  111.3 39.2 all-gather.1
  154.6 329.4 all-reduce.1
where the time goes:
time: 493 us; the launch traced here: 492 us
  waiting for transfers between devices  465 us (94%)
  between operations  13.8 us (3%)
  matrix products  9.78 us (2%)
    psum x1, waiting for transfers between devices, local(): gram_matrix = lax.psum(gram_rows * inverse_count, ('gx', 'gz'))  330 us
    reduce_scatter x1, waiting for transfers between devices, local(): lax.psum_scatter(jnp.einsum('ir,vikj->vrkj', factor, tensor, precision=la...  94.2 us
    all_gather x1, waiting for transfers between devices, local(): lax.all_gather(core_tensor, 'gy', axis=3, tiled=True)  41.3 us
  transfers between devices with their start and end apart: 3, of which 3 were waited for; matrix products, arithmetic and copies ran while one was open for 0% of the time, Pallas kernels for 0%

commit v1 on v0

v1 whole, which is shorter than its diff:
```python
import jax
import jax.numpy as jnp
from jax import lax
from jax.sharding import Mesh, PartitionSpec as P

HIGH = lax.Precision.HIGHEST


def exchange(a, axes):
    return lax.all_to_all(a, axes, 0, 0)


def copies(a, count):
    return jnp.broadcast_to(a[None], (count, *a.shape))


def local(tensor, factor):
    v, i, k, j = tensor.shape
    r = factor.shape[1]
    nx, nzl, ny, nzh, nc = (lax.axis_size(a) for a in ("x", "zl", "y", "zh", "c"))

    share, mine = v // nx, v // (nx * nzl)
    rows = i * r // (k * j)
    field = tensor.reshape(nzl, nx, mine * i, k, j).swapaxes(0, 1).reshape(nx, share * i, k, j)
    sent = jnp.concatenate([field, copies(factor.reshape(rows, k, j), nx)], axis=1)
    got = exchange(sent, "x")
    field = got[:, : share * i].reshape(nx, share, i, k, j)
    rows_of = got[:, share * i :].reshape(nx, i, r)
    products = jnp.einsum("xir,xvikj->vrkj", rows_of, field, precision=HIGH)

    core = exchange(products.reshape(nzl, mine, r, k, j), "zl").sum(axis=0)

    slices = exchange(copies(core, ny), "y")
    gram = jnp.einsum("vrkj,yvrkl->jyl", core, slices, precision=HIGH).reshape(j, ny * j)
    gram = gram * (1.0 / float(v * r * k * nzh * nc))

    group = ("zl", "x", "c")
    count = nzl * nx * nc
    part = exchange(gram.reshape(count, -1, ny * j), group).sum(axis=0)
    part = exchange(copies(part, nzh), "zh").sum(axis=0)
    gram = exchange(copies(part, count), group).reshape(j, ny * j)
    return core, gram


def solution(mesh):
    fine = Mesh(mesh.devices.reshape(4, 4, 4, 4, 2), ("zl", "x", "y", "zh", "c"))
    gx, gz = ("zl", "x"), ("zh", "c")
    in_specs = (P(None, gx, gz, "y"), P(gx, None))
    out_specs = (P(gx, None, gz, "y"), P("y", None))
    return jax.shard_map(local, mesh=fine, in_specs=in_specs, out_specs=out_specs, check_vma=False)
```

time: 493 us -> 144 us (0.29)
  waiting for transfers between devices: 465 us -> 10.3 us
  blocking collectives: 0 us -> 118 us
  between operations: 13.8 us -> 0.74 us
  matrix products: 9.78 us -> 2.09 us
  starting transfers between devices: 0.12 us -> 5.26 us
    psum x1 -> x0, waiting for transfers between devices: 330 us -> none  [local(): gram_matrix = lax.psum(gram_rows * inverse_count, ('gx', 'gz'))]
    all_to_all x0 -> x5, blocking collectives: none -> 118 us  [exchange(): return lax.all_to_all(a, axes, 0, 0)]
    reduce_scatter x1 -> x0, waiting for transfers between devices: 94.2 us -> none  [local(): lax.psum_scatter(jnp.einsum('ir,vikj->vrkj', factor, tensor, precision=la...]
    all_gather x1 -> x0, waiting for transfers between devices: 41.3 us -> none  [local(): lax.all_gather(core_tensor, 'gy', axis=3, tiled=True)]
    all_to_all x0 -> x1, waiting for transfers between devices: none -> 10.3 us  [exchange(): return lax.all_to_all(a, axes, 0, 0)]
    dot_general x2, matrix products: 9.78 us -> 2.09 us  [the longest x1 1.32 us: local(): products = jnp.einsum('xir,xvikj->vrkj', rows_of, field, precision=HIGH)]
    all_to_all x0 -> x1, starting transfers between devices: none -> 5.26 us  [exchange(): return lax.all_to_all(a, axes, 0, 0)]
  transfers between devices with their start and end apart: 3 -> 1, of which waited for: 3 -> 1; matrix products, arithmetic and copies ran while one was open for 0% -> 1% of each run, Pallas kernels for 0% -> 0%
where the time goes in v1:
time: 144 us; the launch traced here: 143 us
  blocking collectives  118 us (82%)
  waiting for transfers between devices  10.3 us (7%)
  local copies, waits for them, and re-layouts  5.7 us (4%)
  starting transfers between devices  5.26 us (4%)
  matrix products  2.09 us (1%)
    all_to_all x5, blocking collectives, exchange(): return lax.all_to_all(a, axes, 0, 0)  118 us
    all_to_all x1, waiting for transfers between devices, exchange(): return lax.all_to_all(a, axes, 0, 0)  10.3 us
    all_to_all x1, starting transfers between devices, exchange(): return lax.all_to_all(a, axes, 0, 0)  5.26 us
  transfers between devices with their start and end apart: 1, of which 1 were waited for; matrix products, arithmetic and copies ran while one was open for 1% of the time, Pallas kernels for 0%

profile of v1, /device:TPU:1, one launch (start us, length us, event | category | flops | bytes accessed | tf_op | source)
XLA Modules:
  0.0 143.1 jit_solution(9511549233566658433)
XLA Ops:
  0.6 0.8 broadcast_in_dim.10
  1.4 1.7 %copy.20 = f32[4,4,64,4,128]{4,3,2,0,1:T(4,128)S(1)} copy(f32[4,4,64,4,128]{4,3,2,1,0:T(4,128)} %bitcast.31) | data formatting | bytes 4194304 | tf_op jit(solution)/shard_map/reshape | solution.py:24
  3.2 0.5 pad_maximum_fusion
  3.7 26.7 %all_to_all.30 = f32[4,260,4,128]{3,2,1,0:T(4,128)S(1)} all-to-all(f32[4,260,4,128]{3,2,1,0:T(4,128)S(1)} %pad_maximum_fusion), channel_id=1, replica_groups=mesh['zl'=4,'x'=4,'y'=4,'zh'=4,'c'=2] {'x'}, dimensions={0} | all-to-all | bytes 4259840 | tf_op jit(solution)/shard_map/all_to_all | solution.py:10
  30.4 0.1 slice.8
  30.5 0.2 copy.31
  30.8 0.1 reshape.38
  30.8 1.3 fusion.3
  32.2 0.1 copy.29
  32.3 33.5 %all_to_all.31 = f32[4,2,64,4,128]{4,2,3,1,0:T(8,128)S(1)} all-to-all(f32[4,2,64,4,128]{4,2,3,1,0:T(8,128)S(1)} %bitcast.30), channel_id=1, replica_groups=mesh['zl'=4,'x'=4,'y'=4,'zh'=4,'c'=2] {'zl'}, dimensions={0} | all-to-all | bytes 2097152 | tf_op jit(solution)/shard_map/all_to_all | solution.py:10
  65.8 0.1 reduce_sum.27
  65.9 0.1 broadcast_in_dim.12
  66.0 16.8 %all_to_all.32 = f32[4,2,64,4,128]{4,2,1,3,0:T(8,128)S(1)} all-to-all(f32[4,2,64,4,128]{4,2,1,3,0:T(8,128)S(1)} %broadcast_in_dim.12), channel_id=1, replica_groups=mesh['zl'=4,'x'=4,'y'=4,'zh'=4,'c'=2] {'y'}, dimensions={0} | all-to-all | bytes 2097152 | tf_op jit(solution)/shard_map/all_to_all | solution.py:10
  82.8 0.8 fusion
  83.5 0.1 reshape.36
  83.6 18.0 %all_to_all.33 = f32[32,4,512]{2,1,0:T(4,128)S(1)} all-to-all(f32[32,4,512]{2,1,0:T(4,128)S(1)} %reshape.36), channel_id=1, replica_groups=mesh['zl'=4,'x'=4,'y'=4,'zh'=4,'c'=2] {'zl','x','c'}, dimensions={0} | all-to-all | bytes 524288 | tf_op jit(solution)/shard_map/all_to_all | solution.py:10
  101.6 0.1 reduce_sum.28
  101.7 23.4 %all_to_all.34 = f32[4,4,512]{2,1,0:T(4,128)S(1)} all-to-all(f32[4,4,512]{2,1,0:T(4,128)S(1)} %broadcast_in_dim.13), channel_id=1, replica_groups=mesh['zl'=4,'x'=4,'y'=4,'zh'=4,'c'=2] {'zh'}, dimensions={0} | all-to-all | bytes 65536 | tf_op jit(solution)/shard_map/all_to_all | solution.py:10
  125.1 0.7 broadcast_in_dim.14
  125.9 5.3 %all-to-all-start.5 = ((f32[32,4,512]{2,1,0:T(4,128)}), f32[32,4,512]{2,1,0:T(4,128)S(1)}, u32[]{:S(2)}, u32[]{:S(2)}) async-start(f32[32,4,512]{2,1,0:T(4,128)} %broadcast_in_dim.14), calls=%async_computation.5 | async-start | bytes 524288 | tf_op jit(solution)/shard_map/all_to_all | solution.py:10
  131.2 0.9 copy.26
  132.0 10.3 %all-to-all-done.5 = f32[32,4,512]{2,1,0:T(4,128)S(1)} async-done(((f32[32,4,512]{2,1,0:T(4,128)}), f32[32,4,512]{2,1,0:T(4,128)S(1)}, u32[]{:S(2)}, u32[]{:S(2)}) %all-to-all-start.5) | async-done | bytes 262176 | tf_op jit(solution)/shard_map/all_to_all | solution.py:10
  142.3 0.8 reshape.37
  (5 shorter events, 0.1 us)
Async XLA Ops:
  125.9 16.4 %all-to-all-start.5 = ((f32[32,4,512]{2,1,0:T(4,128)}), f32[32,4,512]{2,1,0:T(4,128)S(1)}, u32[]{:S(2)}, u32[]{:S(2)}) async-start(f32[32,4,512]{2,1,0:T(4,128)} %broadcast_in_dim.14), calls=%async_computation.5 | async-start | bytes 524288 | tf_op jit(solution)/shard_map/all_to_all | solution.py:10

commit v2 on v1

v2 whole, which is shorter than its diff:
```python
import jax
import jax.numpy as jnp
from jax import lax
from jax.sharding import Mesh, PartitionSpec as P

HIGH = lax.Precision.HIGH
ZL = ("zm", "zn")
LANES = 128
LATE = 3


def exchange(a, axes):
    return lax.all_to_all(a, axes, 0, 0)


def copies(a, count):
    return jnp.broadcast_to(a[None], (count, *a.shape))


def pick(a, index):
    return lax.dynamic_index_in_dim(a, index, 0)


def local(tensor, factor):
    v, i, k, j = tensor.shape
    r = factor.shape[1]
    nx, nzl, ny, nzh, nc = (lax.axis_size(a) for a in ("x", ZL, "y", "zh", "c"))
    me_x, me_z = lax.axis_index("x"), lax.axis_index(ZL)
    mine = v // (nx * nzl)
    slabs = tensor.reshape(nzl, nx, mine, i, k, j).swapaxes(3, 4).reshape(nzl, nx, mine * k, i, j)
    factor = jnp.pad(factor, ((0, 0), (0, LANES - r)))

    late = slabs[:, :, -LATE:].reshape(nzl, -1, j)
    late = jnp.concatenate([late, copies(factor, nzl)], axis=1)
    came = exchange(late, ZL)
    rest = slabs[:, :, :-LATE].swapaxes(0, 1).reshape(nx, -1, j)
    rest = jnp.concatenate([rest, copies(factor, nx)], axis=1)
    got = [pick(rest, me_x)]
    for d in (2, 1, 3):
        got.append(lax.ppermute(pick(rest, (me_x + d) % nx), "x", [(x, (x + d) % nx) for x in range(nx)]))
    got = jnp.concatenate(got)

    def product(got):
        field = got[:, :-i].reshape(nx, -1, i, j)
        return jnp.einsum("xir,xuij->urj", got[:, -i:, :r], field, precision=HIGH)

    products = product(got).reshape(nzl, -1, r, j)
    products, came = lax.optimization_barrier((products, came))
    other = product(came).reshape(nx, -1, r, j)

    sums = exchange(products, ZL).sum(axis=0)
    tail = pick(other, me_x)[0]
    for d in (2, 1, 3):
        tail = tail + lax.ppermute(pick(other, (me_x + d) % nx), "x", [(x, (x + d) % nx) for x in range(nx)])[0]
    core = jnp.concatenate([sums, tail]).reshape(-1, j)

    slices = exchange(copies(core, ny), "y")
    gram = jnp.einsum("aj,yal->jyl", core, slices, precision=HIGH).reshape(j, ny * j)
    gram = gram * (1.0 / float(v * r * k * nzh * nc))

    near, far = ("x", "c", "zn"), ("zm", "zh")
    count, others = nx * nc * nzl // 2, 2 * nzh
    part = exchange(gram.reshape(count, -1, ny * j), near).sum(axis=0)
    part = exchange(copies(part, others), far).sum(axis=0)
    gram = exchange(copies(part, count), near).reshape(j, ny * j)
    return core.reshape(mine, k, r, j).swapaxes(1, 2), gram


def solution(mesh):
    fine = Mesh(mesh.devices.reshape(2, 2, 4, 4, 4, 2), ("zm", "zn", "x", "y", "zh", "c"))
    gx, gz = (*ZL, "x"), ("zh", "c")
    in_specs = (P(None, gx, gz, "y"), P(gx, None))
    out_specs = (P(gx, None, gz, "y"), P("y", None))
    return jax.shard_map(local, mesh=fine, in_specs=in_specs, out_specs=out_specs, check_vma=False)
```

time: 144 us -> 129 us (0.90)
  blocking collectives: 118 us -> 58 us
  starting transfers between devices: 5.26 us -> 39.6 us
  waiting for transfers between devices: 10.3 us -> 18.6 us
    all_to_all x5 -> x3, blocking collectives: 118 us -> 58 us  [exchange(): return lax.all_to_all(a, axes, 0, 0)]
    ppermute x0 -> x6, starting transfers between devices: none -> 21.6 us  [the longest x3 11.1 us: local(): lax.ppermute(pick(rest, (me_x + d) % nx), 'x', [(x, (x + d) % nx) for x i...]
    all_to_all x1 -> x3, starting transfers between devices: 5.26 us -> 18 us  [exchange(): return lax.all_to_all(a, axes, 0, 0)]
    ppermute x0 -> x6, waiting for transfers between devices: none -> 12 us  [the longest x3 8.67 us: local(): lax.ppermute(pick(rest, (me_x + d) % nx), 'x', [(x, (x + d) % nx) for x i...]
    all_to_all x1 -> x3, waiting for transfers between devices: 10.3 us -> 6.55 us  [exchange(): return lax.all_to_all(a, axes, 0, 0)]
    reshape x4 -> x1, local copies, waits for them, and re-layouts: 2.69 us -> 0.13 us  [local(): core = jnp.concatenate([sums, tail]).reshape(-1, j)]
    transpose x0 -> x1, local copies, waits for them, and re-layouts: none -> 1.84 us  [local(): tensor.reshape(nzl, nx, mine, i, k, j).swapaxes(3, 4)]
    dot_general x2 -> x3, matrix products: 2.09 us -> 3.28 us  [the longest x2 2.55 us: product(): return jnp.einsum('xir,xuij->urj', got[:, -i:, :r], field, precision=HIGH)]
  transfers between devices with their start and end apart: 1 -> 9, of which waited for: 1 -> 5; matrix products, arithmetic and copies ran while one was open for 1% -> 4% of each run, Pallas kernels for 0% -> 0%
where the time goes in v2:
time: 129 us; the launch traced here: 128 us
  blocking collectives  58 us (45%)
  starting transfers between devices  39.6 us (31%)
  waiting for transfers between devices  18.6 us (14%)
  local copies, waits for them, and re-layouts  6.57 us (5%)
  matrix products  3.28 us (3%)
  other arithmetic  1.34 us (1%)
    all_to_all x3, blocking collectives, exchange(): return lax.all_to_all(a, axes, 0, 0)  58 us
    all_to_all x3, starting transfers between devices, exchange(): return lax.all_to_all(a, axes, 0, 0)  18 us
    ppermute x3, starting transfers between devices, local(): lax.ppermute(pick(rest, (me_x + d) % nx), 'x', [(x, (x + d) % nx) for x i...  11.1 us
    ppermute x3, starting transfers between devices, local(): lax.ppermute(pick(other, (me_x + d) % nx), 'x', [(x, (x + d) % nx) for x...  10.4 us
    ppermute x3, waiting for transfers between devices, local(): lax.ppermute(pick(rest, (me_x + d) % nx), 'x', [(x, (x + d) % nx) for x i...  8.67 us
    all_to_all x3, waiting for transfers between devices, exchange(): return lax.all_to_all(a, axes, 0, 0)  6.55 us
    ppermute x3, waiting for transfers between devices, local(): lax.ppermute(pick(other, (me_x + d) % nx), 'x', [(x, (x + d) % nx) for x...  3.33 us
  transfers between devices with their start and end apart: 9, of which 5 were waited for; matrix products, arithmetic and copies ran while one was open for 4% of the time, Pallas kernels for 0%

profile of v2, /device:TPU:1, one launch (start us, length us, event | category | flops | bytes accessed | tf_op | source)
XLA Modules:
  0.0 128.1 jit_solution(1808278628913989760)
XLA Ops:
  0.6 1.8 %copy.14 = f32[4,4,2,4,32,128]{5,4,3,2,0,1:T(8,128)S(1)} copy(f32[4,4,2,4,32,128]{5,3,4,2,1,0:T(4,128)} %bitcast.56) | data formatting | bytes 4194304 | tf_op jit(solution)/shard_map/transpose | solution.py:30
  3.2 1.0 pad_maximum_fusion.1
  4.2 6.4 %all-to-all-start = ((f32[4,416,128]{2,1,0:T(8,128)}), f32[4,416,128]{2,1,0:T(8,128)}, u32[]{:S(2)}, u32[]{:S(2)}) async-start(f32[4,416,128]{2,1,0:T(8,128)} %pad_maximum_fusion.1), calls=%async_computation | async-start | bytes 1703936 | tf_op jit(solution)/shard_map/all_to_all | solution.py:13
  11.0 4.7 %collective-permute-start = (f32[1,672,128]{2,1,0:T(8,128)S(1)}, f32[1,672,128]{2,1,0:T(8,128)S(1)}, u32[]{:S(2)}, u32[]{:S(2)}) collective-permute-start(f32[1,672,128]{2,1,0:T(8,128)S(1)} %get-tuple-element.11), channel_id=1, source_target_pairs={{0,64},{32,96},{64,0},{96,32},{1,65},{33,97},{65,1},{97,33},{2,66}... | collective-permute-start | bytes 1032200 | tf_op jit(solution)/shard_map/ppermute | solution.py:40
  15.6 2.2 %collective-permute-start.1 = (f32[1,672,128]{2,1,0:T(8,128)S(1)}, f32[1,672,128]{2,1,0:T(8,128)S(1)}, u32[]{:S(2)}, u32[]{:S(2)}) collective-permute-start(f32[1,672,128]{2,1,0:T(8,128)S(1)} %get-tuple-element.12), channel_id=1, source_target_pairs={{0,32},{32,64},{64,96},{96,0},{1,33},{33,65},{65,97},{97,1},{2,34}... | collective-permute-start | bytes 1032200 | tf_op jit(solution)/shard_map/ppermute | solution.py:40
  17.8 4.3 %collective-permute-start.2 = (f32[1,672,128]{2,1,0:T(8,128)S(1)}, f32[1,672,128]{2,1,0:T(8,128)S(1)}, u32[]{:S(2)}, u32[]{:S(2)}) collective-permute-start(f32[1,672,128]{2,1,0:T(8,128)S(1)} %get-tuple-element.13), channel_id=1, source_target_pairs={{0,96},{32,0},{64,32},{96,64},{1,97},{33,1},{65,33},{97,65},{2,98}... | collective-permute-start | bytes 1032200 | tf_op jit(solution)/shard_map/ppermute | solution.py:40
  22.1 8.7 %collective-permute-done.1 = f32[1,672,128]{2,1,0:T(8,128)S(1)} collective-permute-done((f32[1,672,128]{2,1,0:T(8,128)S(1)}, f32[1,672,128]{2,1,0:T(8,128)S(1)}, u32[]{:S(2)}, u32[]{:S(2)}) %collective-permute-start.1) | collective-permute-done | bytes 344096 | tf_op jit(solution)/shard_map/ppermute | solution.py:40
  31.0 1.3 %fusion.5 = f32[20,128,64,1]{1,2,0,3:T(8,128)} fusion(f32[4,20,32,128]{3,2,1,0:T(8,128)S(1)} %bitcast.48, f32[1,672,128]{2,1,0:T(8,128)S(1)} %collective-permute-done.2, f32[1,672,128]{2,1,0:T(8,128)S(1)} %collective-permute-done.1, f32[1,672,128]{2,1,0:T(8,128)S(1)} %collective-permute-done, f32[1,672,128]{2,1,0:T(8,128)S(1)} %get-tuple-element.10), kind=kOutput, calls=%fused_computation.19 | convolution fusion | flops 125853696 | bytes 3342336 | tf_op jit(solution)/shard_map/xir,xuij->urj/dot_general | solution.py:45
  32.3 4.3 %all-to-all-start.1 = ((f32[4,5,64,128]{3,2,1,0:T(8,128)}), f32[4,5,64,128]{3,2,1,0:T(8,128)S(1)}, u32[]{:S(2)}, u32[]{:S(2)}) async-start(f32[4,5,64,128]{3,2,1,0:T(8,128)} %bitcast.10), calls=%async_computation.1 | async-start | bytes 1310720 | tf_op jit(solution)/shard_map/all_to_all | solution.py:13
  36.7 1.2 slice.22
  37.9 1.2 fusion.12
  39.1 5.1 %collective-permute-start.3 = (f32[1,3,64,128]{3,2,1,0:T(8,128)S(1)}, f32[1,3,64,128]{3,2,1,0:T(8,128)S(1)}, u32[]{:S(2)}, u32[]{:S(2)}) collective-permute-start(f32[1,3,64,128]{3,2,1,0:T(8,128)S(1)} %get-tuple-element.14), channel_id=1, source_target_pairs={{0,64},{32,96},{64,0},{96,32},{1,65},{33,97},{65,1},{97,33},{2,66}... | collective-permute-start | bytes 294920 | tf_op jit(solution)/shard_map/ppermute | solution.py:54
  44.3 1.9 %collective-permute-start.5 = (f32[1,3,64,128]{3,2,1,0:T(8,128)S(1)}, f32[1,3,64,128]{3,2,1,0:T(8,128)S(1)}, u32[]{:S(2)}, u32[]{:S(2)}) collective-permute-start(f32[1,3,64,128]{3,2,1,0:T(8,128)S(1)} %get-tuple-element.15), channel_id=1, source_target_pairs={{0,96},{32,0},{64,32},{96,64},{1,97},{33,1},{65,33},{97,65},{2,98}... | collective-permute-start | bytes 294920 | tf_op jit(solution)/shard_map/ppermute | solution.py:54
  46.2 3.4 %collective-permute-start.4 = (f32[1,3,64,128]{3,2,1,0:T(8,128)S(1)}, f32[1,3,64,128]{3,2,1,0:T(8,128)S(1)}, u32[]{:S(2)}, u32[]{:S(2)}) collective-permute-start(f32[1,3,64,128]{3,2,1,0:T(8,128)S(1)} %get-tuple-element.16), channel_id=1, source_target_pairs={{0,32},{32,64},{64,96},{96,0},{1,33},{33,65},{65,97},{97,1},{2,34}... | collective-permute-start | bytes 294920 | tf_op jit(solution)/shard_map/ppermute | solution.py:54
  49.9 3.0 %collective-permute-done.4 = f32[1,3,64,128]{3,2,1,0:T(8,128)S(1)} collective-permute-done((f32[1,3,64,128]{3,2,1,0:T(8,128)S(1)}, f32[1,3,64,128]{3,2,1,0:T(8,128)S(1)}, u32[]{:S(2)}, u32[]{:S(2)}) %collective-permute-start.4) | collective-permute-done | bytes 98336 | tf_op jit(solution)/shard_map/ppermute | solution.py:54
  53.5 17.1 %all_to_all.30 = f32[4,512,128]{1,2,0:T(8,128)S(1)} all-to-all(f32[4,512,128]{1,2,0:T(8,128)S(1)} %broadcast_in_dim.9), channel_id=1, replica_groups=mesh['zm'=2,'zn'=2,'x'=4,'y'=4,'zh'=4,'c'=2] {'y'}, dimensions={0} | all-to-all | bytes 2097152 | tf_op jit(solution)/shard_map/all_to_all | solution.py:13
  70.6 0.7 fusion
  71.4 15.6 %all_to_all.31 = f32[16,8,512]{2,1,0:T(8,128)S(1)} all-to-all(f32[16,8,512]{2,1,0:T(8,128)S(1)} %fusion), channel_id=1, replica_groups=mesh['zm'=2,'zn'=2,'x'=4,'y'=4,'zh'=4,'c'=2] {'x','c','zn'}, dimensions={0} | all-to-all | bytes 524288 | tf_op jit(solution)/shard_map/all_to_all | solution.py:13
  87.0 25.2 %all_to_all.32 = f32[8,8,512]{2,1,0:T(8,128)S(1)} all-to-all(f32[8,8,512]{2,1,0:T(8,128)S(1)} %broadcast_in_dim.10), channel_id=1, replica_groups=mesh['zm'=2,'zn'=2,'x'=4,'y'=4,'zh'=4,'c'=2] {'zm','zh'}, dimensions={0} | all-to-all | bytes 262144 | tf_op jit(solution)/shard_map/all_to_all | solution.py:13
  112.3 0.7 broadcast_in_dim.11
  113.0 7.2 %all-to-all-start.5 = ((f32[16,8,512]{2,1,0:T(8,128)}), f32[16,8,512]{2,1,0:T(8,128)S(1)}, u32[]{:S(2)}, u32[]{:S(2)}) async-start(f32[16,8,512]{2,1,0:T(8,128)} %broadcast_in_dim.11), calls=%async_computation.5 | async-start | bytes 524288 | tf_op jit(solution)/shard_map/all_to_all | solution.py:13
  120.2 0.9 copy.17
  121.1 6.3 %all-to-all-done.5 = f32[16,8,512]{2,1,0:T(8,128)S(1)} async-done(((f32[16,8,512]{2,1,0:T(8,128)}), f32[16,8,512]{2,1,0:T(8,128)S(1)}, u32[]{:S(2)}, u32[]{:S(2)}) %all-to-all-start.5) | async-done | bytes 262176 | tf_op jit(solution)/shard_map/all_to_all | solution.py:13
  127.4 0.7 copy.21
  (25 shorter events, 2.1 us)
Async XLA Ops:
  2.5 0.7 copy-start
  4.2 28.1 %all-to-all-start = ((f32[4,416,128]{2,1,0:T(8,128)}), f32[4,416,128]{2,1,0:T(8,128)}, u32[]{:S(2)}, u32[]{:S(2)}) async-start(f32[4,416,128]{2,1,0:T(8,128)} %pad_maximum_fusion.1), calls=%async_computation | async-start | bytes 1703936 | tf_op jit(solution)/shard_map/all_to_all | solution.py:13
  11.0 11.2 %collective-permute-start = (f32[1,672,128]{2,1,0:T(8,128)S(1)}, f32[1,672,128]{2,1,0:T(8,128)S(1)}, u32[]{:S(2)}, u32[]{:S(2)}) collective-permute-start(f32[1,672,128]{2,1,0:T(8,128)S(1)} %get-tuple-element.11), channel_id=1, source_target_pairs={{0,64},{32,96},{64,0},{96,32},{1,65},{33,97},{65,1},{97,33},{2,66}... | collective-permute-start | bytes 1032200 | tf_op jit(solution)/shard_map/ppermute | solution.py:40
  15.6 15.2 %collective-permute-start.1 = (f32[1,672,128]{2,1,0:T(8,128)S(1)}, f32[1,672,128]{2,1,0:T(8,128)S(1)}, u32[]{:S(2)}, u32[]{:S(2)}) collective-permute-start(f32[1,672,128]{2,1,0:T(8,128)S(1)} %get-tuple-element.12), channel_id=1, source_target_pairs={{0,32},{32,64},{64,96},{96,0},{1,33},{33,65},{65,97},{97,1},{2,34}... | collective-permute-start | bytes 1032200 | tf_op jit(solution)/shard_map/ppermute | solution.py:40
  17.8 13.0 %collective-permute-start.2 = (f32[1,672,128]{2,1,0:T(8,128)S(1)}, f32[1,672,128]{2,1,0:T(8,128)S(1)}, u32[]{:S(2)}, u32[]{:S(2)}) collective-permute-start(f32[1,672,128]{2,1,0:T(8,128)S(1)} %get-tuple-element.13), channel_id=1, source_target_pairs={{0,96},{32,0},{64,32},{96,64},{1,97},{33,1},{65,33},{97,65},{2,98}... | collective-permute-start | bytes 1032200 | tf_op jit(solution)/shard_map/ppermute | solution.py:40
  32.3 20.9 %all-to-all-start.1 = ((f32[4,5,64,128]{3,2,1,0:T(8,128)}), f32[4,5,64,128]{3,2,1,0:T(8,128)S(1)}, u32[]{:S(2)}, u32[]{:S(2)}) async-start(f32[4,5,64,128]{3,2,1,0:T(8,128)} %bitcast.10), calls=%async_computation.1 | async-start | bytes 1310720 | tf_op jit(solution)/shard_map/all_to_all | solution.py:13
  39.1 10.4 %collective-permute-start.3 = (f32[1,3,64,128]{3,2,1,0:T(8,128)S(1)}, f32[1,3,64,128]{3,2,1,0:T(8,128)S(1)}, u32[]{:S(2)}, u32[]{:S(2)}) collective-permute-start(f32[1,3,64,128]{3,2,1,0:T(8,128)S(1)} %get-tuple-element.14), channel_id=1, source_target_pairs={{0,64},{32,96},{64,0},{96,32},{1,65},{33,97},{65,1},{97,33},{2,66}... | collective-permute-start | bytes 294920 | tf_op jit(solution)/shard_map/ppermute | solution.py:54
  44.3 5.6 %collective-permute-start.5 = (f32[1,3,64,128]{3,2,1,0:T(8,128)S(1)}, f32[1,3,64,128]{3,2,1,0:T(8,128)S(1)}, u32[]{:S(2)}, u32[]{:S(2)}) collective-permute-start(f32[1,3,64,128]{3,2,1,0:T(8,128)S(1)} %get-tuple-element.15), channel_id=1, source_target_pairs={{0,96},{32,0},{64,32},{96,64},{1,97},{33,1},{65,33},{97,65},{2,98}... | collective-permute-start | bytes 294920 | tf_op jit(solution)/shard_map/ppermute | solution.py:54
  46.2 6.7 %collective-permute-start.4 = (f32[1,3,64,128]{3,2,1,0:T(8,128)S(1)}, f32[1,3,64,128]{3,2,1,0:T(8,128)S(1)}, u32[]{:S(2)}, u32[]{:S(2)}) collective-permute-start(f32[1,3,64,128]{3,2,1,0:T(8,128)S(1)} %get-tuple-element.16), channel_id=1, source_target_pairs={{0,32},{32,64},{64,96},{96,0},{1,33},{33,65},{65,97},{97,1},{2,34}... | collective-permute-start | bytes 294920 | tf_op jit(solution)/shard_map/ppermute | solution.py:54
  113.0 14.4 %all-to-all-start.5 = ((f32[16,8,512]{2,1,0:T(8,128)}), f32[16,8,512]{2,1,0:T(8,128)S(1)}, u32[]{:S(2)}, u32[]{:S(2)}) async-start(f32[16,8,512]{2,1,0:T(8,128)} %broadcast_in_dim.11), calls=%async_computation.5 | async-start | bytes 524288 | tf_op jit(solution)/shard_map/all_to_all | solution.py:13

commit v3 on v2

--- a/solution.py
+++ b/solution.py
@@ -27,16 +27,18 @@
     nx, nzl, ny, nzh, nc = (lax.axis_size(a) for a in ("x", ZL, "y", "zh", "c"))
     me_x, me_z = lax.axis_index("x"), lax.axis_index(ZL)
     mine = v // (nx * nzl)
+    late = tensor.reshape(nzl, nx, mine, i, k, j)[:, :, 1, :, k - LATE :].swapaxes(2, 3)
+    late, tensor = lax.optimization_barrier((late, tensor))
     slabs = tensor.reshape(nzl, nx, mine, i, k, j).swapaxes(3, 4).reshape(nzl, nx, mine * k, i, j)
     factor = jnp.pad(factor, ((0, 0), (0, LANES - r)))
 
-    late = slabs[:, :, -LATE:].reshape(nzl, -1, j)
+    late = late.reshape(nzl, -1, j)
     late = jnp.concatenate([late, copies(factor, nzl)], axis=1)
     came = exchange(late, ZL)
     rest = slabs[:, :, :-LATE].swapaxes(0, 1).reshape(nx, -1, j)
     rest = jnp.concatenate([rest, copies(factor, nx)], axis=1)
     got = [pick(rest, me_x)]
-    for d in (2, 1, 3):
+    for d in (1, 3, 2):
         got.append(lax.ppermute(pick(rest, (me_x + d) % nx), "x", [(x, (x + d) % nx) for x in range(nx)]))
     got = jnp.concatenate(got)
 

time: 129 us -> 127 us (0.984)
    transpose x1, local copies, waits for them, and re-layouts: 1.84 us -> 0.25 us  [local(): tensor.reshape(nzl, nx, mine, i, k, j).swapaxes(3, 4)]
    ppermute x3, waiting for transfers between devices: 3.33 us -> 4.77 us  [local(): lax.ppermute(pick(other, (me_x + d) % nx), 'x', [(x, (x + d) % nx) for x...]
    slice x2 -> x1, local copies, waits for them, and re-layouts: 0.11 us -> 1.51 us  [local(): tensor.reshape(nzl, nx, mine, i, k, j)[:, :, 1, :, k - LATE:].swapaxes(2, 3)]
  transfers between devices with their start and end apart: 9 -> 9, of which waited for: 5 -> 4; matrix products, arithmetic and copies ran while one was open for 4% -> 3% of each run, Pallas kernels for 0% -> 0%
where the time goes in v3:
time: 127 us
  blocking collectives  58.4 us (46%)
  starting transfers between devices  39.1 us (31%)
  waiting for transfers between devices  19.1 us (15%)
  local copies, waits for them, and re-layouts  5.33 us (4%)
  matrix products  2.42 us (2%)
  other arithmetic  1.3 us (1%)
    all_to_all x3, blocking collectives, exchange(): return lax.all_to_all(a, axes, 0, 0)  58.4 us
    all_to_all x3, starting transfers between devices, exchange(): return lax.all_to_all(a, axes, 0, 0)  17.7 us
    ppermute x3, starting transfers between devices, local(): lax.ppermute(pick(other, (me_x + d) % nx), 'x', [(x, (x + d) % nx) for x...  11.4 us
    ppermute x3, starting transfers between devices, local(): lax.ppermute(pick(rest, (me_x + d) % nx), 'x', [(x, (x + d) % nx) for x i...  9.93 us
    ppermute x3, waiting for transfers between devices, local(): lax.ppermute(pick(rest, (me_x + d) % nx), 'x', [(x, (x + d) % nx) for x i...  8.05 us
    all_to_all x3, waiting for transfers between devices, exchange(): return lax.all_to_all(a, axes, 0, 0)  6.3 us
    ppermute x3, waiting for transfers between devices, local(): lax.ppermute(pick(other, (me_x + d) % nx), 'x', [(x, (x + d) % nx) for x...  4.77 us
  transfers between devices with their start and end apart: 9, of which 4 were waited for; matrix products, arithmetic and copies ran while one was open for 3% of the time, Pallas kernels for 0%

profile of v3, /device:TPU:1, one launch (start us, length us, event | category | flops | bytes accessed | tf_op | source)
XLA Modules:
  0.0 126.5 jit_solution(10446520808235997087)
XLA Ops:
  0.6 1.5 %slice.24 = f32[4,4,1,32,3,128]{5,4,3,2,1,0:T(4,128)S(1)} slice(f32[4,4,2,32,4,128]{5,4,3,2,1,0:T(4,128)} %bitcast.55), slice={[0:4], [0:4], [1:2], [0:32], [1:4], [0:128]} | slice | bytes 1572864 | tf_op jit(solution)/shard_map/slice | solution.py:30
  2.2 0.6 copy-done.1
  2.9 1.0 pad_maximum_fusion.1
  3.9 6.4 %all-to-all-start = ((f32[4,416,128]{2,1,0:T(8,128)}), f32[4,416,128]{2,1,0:T(8,128)S(1)}, u32[]{:S(2)}, u32[]{:S(2)}) async-start(f32[4,416,128]{2,1,0:T(8,128)} %pad_maximum_fusion.1), calls=%async_computation | async-start | bytes 1703936 | tf_op jit(solution)/shard_map/all_to_all | solution.py:13
  10.8 3.1 %collective-permute-start = (f32[1,672,128]{2,1,0:T(8,128)S(1)}, f32[1,672,128]{2,1,0:T(8,128)S(1)}, u32[]{:S(2)}, u32[]{:S(2)}) collective-permute-start(f32[1,672,128]{2,1,0:T(8,128)S(1)} %get-tuple-element.15), channel_id=1, source_target_pairs={{0,32},{32,64},{64,96},{96,0},{1,33},{33,65},{65,97},{97,1},{2,34}... | collective-permute-start | bytes 1032200 | tf_op jit(solution)/shard_map/ppermute | solution.py:42
  13.9 3.4 %collective-permute-start.1 = (f32[1,672,128]{2,1,0:T(8,128)S(1)}, f32[1,672,128]{2,1,0:T(8,128)S(1)}, u32[]{:S(2)}, u32[]{:S(2)}) collective-permute-start(f32[1,672,128]{2,1,0:T(8,128)S(1)} %get-tuple-element.16), channel_id=1, source_target_pairs={{0,96},{32,0},{64,32},{96,64},{1,97},{33,1},{65,33},{97,65},{2,98}... | collective-permute-start | bytes 1032200 | tf_op jit(solution)/shard_map/ppermute | solution.py:42
  17.3 3.4 %collective-permute-start.2 = (f32[1,672,128]{2,1,0:T(8,128)S(1)}, f32[1,672,128]{2,1,0:T(8,128)S(1)}, u32[]{:S(2)}, u32[]{:S(2)}) collective-permute-start(f32[1,672,128]{2,1,0:T(8,128)S(1)} %get-tuple-element.17), channel_id=1, source_target_pairs={{0,64},{32,96},{64,0},{96,32},{1,65},{33,97},{65,1},{97,33},{2,66}... | collective-permute-start | bytes 1032200 | tf_op jit(solution)/shard_map/ppermute | solution.py:42
  20.8 1.8 %collective-permute-done.1 = f32[1,672,128]{2,1,0:T(8,128)S(1)} collective-permute-done((f32[1,672,128]{2,1,0:T(8,128)S(1)}, f32[1,672,128]{2,1,0:T(8,128)S(1)}, u32[]{:S(2)}, u32[]{:S(2)}) %collective-permute-start.1) | collective-permute-done | bytes 344096 | tf_op jit(solution)/shard_map/ppermute | solution.py:42
  22.6 6.2 %collective-permute-done.2 = f32[1,672,128]{2,1,0:T(8,128)S(1)} collective-permute-done((f32[1,672,128]{2,1,0:T(8,128)S(1)}, f32[1,672,128]{2,1,0:T(8,128)S(1)}, u32[]{:S(2)}, u32[]{:S(2)}) %collective-permute-start.2) | collective-permute-done | bytes 344096 | tf_op jit(solution)/shard_map/ppermute | solution.py:42
  29.0 1.3 %fusion.5 = f32[20,128,64,1]{1,2,0,3:T(8,128)} fusion(f32[4,20,32,128]{3,2,1,0:T(8,128)S(1)} %bitcast.53, f32[1,672,128]{2,1,0:T(8,128)S(1)} %collective-permute-done.2, f32[1,672,128]{2,1,0:T(8,128)S(1)} %collective-permute-done.1, f32[1,672,128]{2,1,0:T(8,128)S(1)} %collective-permute-done, f32[1,672,128]{2,1,0:T(8,128)S(1)} %get-tuple-element.14), kind=kOutput, calls=%fused_computation.20 | convolution fusion | flops 125853696 | bytes 3342336 | tf_op jit(solution)/shard_map/xir,xuij->urj/dot_general | solution.py:47
  30.4 4.1 %all-to-all-start.1 = ((f32[4,5,64,128]{3,2,1,0:T(8,128)}), f32[4,5,64,128]{3,2,1,0:T(8,128)S(1)}, u32[]{:S(2)}, u32[]{:S(2)}) async-start(f32[4,5,64,128]{3,2,1,0:T(8,128)} %bitcast.13), calls=%async_computation.1 | async-start | bytes 1310720 | tf_op jit(solution)/shard_map/all_to_all | solution.py:13
  34.9 5.0 %collective-permute-start.3 = (f32[1,3,64,128]{3,2,1,0:T(8,128)S(1)}, f32[1,3,64,128]{3,2,1,0:T(8,128)S(1)}, u32[]{:S(2)}, u32[]{:S(2)}) collective-permute-start(f32[1,3,64,128]{3,2,1,0:T(8,128)S(1)} %get-tuple-element.18), channel_id=1, source_target_pairs={{0,64},{32,96},{64,0},{96,32},{1,65},{33,97},{65,1},{97,33},{2,66}... | collective-permute-start | bytes 294920 | tf_op jit(solution)/shard_map/ppermute | solution.py:56
  40.0 4.5 %collective-permute-start.5 = (f32[1,3,64,128]{3,2,1,0:T(8,128)S(1)}, f32[1,3,64,128]{3,2,1,0:T(8,128)S(1)}, u32[]{:S(2)}, u32[]{:S(2)}) collective-permute-start(f32[1,3,64,128]{3,2,1,0:T(8,128)S(1)} %get-tuple-element.19), channel_id=1, source_target_pairs={{0,96},{32,0},{64,32},{96,64},{1,97},{33,1},{65,33},{97,65},{2,98}... | collective-permute-start | bytes 294920 | tf_op jit(solution)/shard_map/ppermute | solution.py:56
  44.4 1.9 %collective-permute-start.4 = (f32[1,3,64,128]{3,2,1,0:T(8,128)S(1)}, f32[1,3,64,128]{3,2,1,0:T(8,128)S(1)}, u32[]{:S(2)}, u32[]{:S(2)}) collective-permute-start(f32[1,3,64,128]{3,2,1,0:T(8,128)S(1)} %get-tuple-element.20), channel_id=1, source_target_pairs={{0,32},{32,64},{64,96},{96,0},{1,33},{33,65},{65,97},{97,1},{2,34}... | collective-permute-start | bytes 294920 | tf_op jit(solution)/shard_map/ppermute | solution.py:56
  46.4 4.8 %collective-permute-done.4 = f32[1,3,64,128]{3,2,1,0:T(8,128)S(1)} collective-permute-done((f32[1,3,64,128]{3,2,1,0:T(8,128)S(1)}, f32[1,3,64,128]{3,2,1,0:T(8,128)S(1)}, u32[]{:S(2)}, u32[]{:S(2)}) %collective-permute-start.4) | collective-permute-done | bytes 98336 | tf_op jit(solution)/shard_map/ppermute | solution.py:56
  51.5 17.7 %all_to_all.30 = f32[4,512,128]{1,2,0:T(8,128)S(1)} all-to-all(f32[4,512,128]{1,2,0:T(8,128)S(1)} %broadcast_in_dim.9), channel_id=1, replica_groups=mesh['zm'=2,'zn'=2,'x'=4,'y'=4,'zh'=4,'c'=2] {'y'}, dimensions={0} | all-to-all | bytes 2097152 | tf_op jit(solution)/shard_map/all_to_all | solution.py:13
  69.3 0.7 fusion
  70.0 15.5 %all_to_all.31 = f32[16,8,512]{2,1,0:T(8,128)S(1)} all-to-all(f32[16,8,512]{2,1,0:T(8,128)S(1)} %fusion), channel_id=1, replica_groups=mesh['zm'=2,'zn'=2,'x'=4,'y'=4,'zh'=4,'c'=2] {'x','c','zn'}, dimensions={0} | all-to-all | bytes 524288 | tf_op jit(solution)/shard_map/all_to_all | solution.py:13
  85.5 25.1 %all_to_all.32 = f32[8,8,512]{2,1,0:T(8,128)S(1)} all-to-all(f32[8,8,512]{2,1,0:T(8,128)S(1)} %broadcast_in_dim.10), channel_id=1, replica_groups=mesh['zm'=2,'zn'=2,'x'=4,'y'=4,'zh'=4,'c'=2] {'zm','zh'}, dimensions={0} | all-to-all | bytes 262144 | tf_op jit(solution)/shard_map/all_to_all | solution.py:13
  110.7 0.7 broadcast_in_dim.11
  111.4 7.2 %all-to-all-start.5 = ((f32[16,8,512]{2,1,0:T(8,128)}), f32[16,8,512]{2,1,0:T(8,128)S(1)}, u32[]{:S(2)}, u32[]{:S(2)}) async-start(f32[16,8,512]{2,1,0:T(8,128)} %broadcast_in_dim.11), calls=%async_computation.5 | async-start | bytes 524288 | tf_op jit(solution)/shard_map/all_to_all | solution.py:13
  118.6 0.9 copy.17
  119.5 6.3 %all-to-all-done.5 = f32[16,8,512]{2,1,0:T(8,128)S(1)} async-done(((f32[16,8,512]{2,1,0:T(8,128)}), f32[16,8,512]{2,1,0:T(8,128)S(1)}, u32[]{:S(2)}, u32[]{:S(2)}) %all-to-all-start.5) | async-done | bytes 262176 | tf_op jit(solution)/shard_map/all_to_all | solution.py:13
  125.8 0.7 copy.24
  (27 shorter events, 1.6 us)
Async XLA Ops:
  2.1 0.7 copy-start.1
  2.9 7.4 %copy-start = (f32[32,32,4,128]{3,2,1,0:T(4,128)S(1)}, f32[32,32,4,128]{3,2,1,0:T(4,128)}, u32[]{:S(2)}) copy-start(f32[32,32,4,128]{3,2,1,0:T(4,128)} %param.2) | copy-start | bytes 6291460
  3.9 26.5 %all-to-all-start = ((f32[4,416,128]{2,1,0:T(8,128)}), f32[4,416,128]{2,1,0:T(8,128)S(1)}, u32[]{:S(2)}, u32[]{:S(2)}) async-start(f32[4,416,128]{2,1,0:T(8,128)} %pad_maximum_fusion.1), calls=%async_computation | async-start | bytes 1703936 | tf_op jit(solution)/shard_map/all_to_all | solution.py:13
  10.8 10.0 %collective-permute-start = (f32[1,672,128]{2,1,0:T(8,128)S(1)}, f32[1,672,128]{2,1,0:T(8,128)S(1)}, u32[]{:S(2)}, u32[]{:S(2)}) collective-permute-start(f32[1,672,128]{2,1,0:T(8,128)S(1)} %get-tuple-element.15), channel_id=1, source_target_pairs={{0,32},{32,64},{64,96},{96,0},{1,33},{33,65},{65,97},{97,1},{2,34}... | collective-permute-start | bytes 1032200 | tf_op jit(solution)/shard_map/ppermute | solution.py:42
  13.9 8.7 %collective-permute-start.1 = (f32[1,672,128]{2,1,0:T(8,128)S(1)}, f32[1,672,128]{2,1,0:T(8,128)S(1)}, u32[]{:S(2)}, u32[]{:S(2)}) collective-permute-start(f32[1,672,128]{2,1,0:T(8,128)S(1)} %get-tuple-element.16), channel_id=1, source_target_pairs={{0,96},{32,0},{64,32},{96,64},{1,97},{33,1},{65,33},{97,65},{2,98}... | collective-permute-start | bytes 1032200 | tf_op jit(solution)/shard_map/ppermute | solution.py:42
  17.3 11.5 %collective-permute-start.2 = (f32[1,672,128]{2,1,0:T(8,128)S(1)}, f32[1,672,128]{2,1,0:T(8,128)S(1)}, u32[]{:S(2)}, u32[]{:S(2)}) collective-permute-start(f32[1,672,128]{2,1,0:T(8,128)S(1)} %get-tuple-element.17), channel_id=1, source_target_pairs={{0,64},{32,96},{64,0},{96,32},{1,65},{33,97},{65,1},{97,33},{2,66}... | collective-permute-start | bytes 1032200 | tf_op jit(solution)/shard_map/ppermute | solution.py:42
  30.4 20.8 %all-to-all-start.1 = ((f32[4,5,64,128]{3,2,1,0:T(8,128)}), f32[4,5,64,128]{3,2,1,0:T(8,128)S(1)}, u32[]{:S(2)}, u32[]{:S(2)}) async-start(f32[4,5,64,128]{3,2,1,0:T(8,128)} %bitcast.13), calls=%async_computation.1 | async-start | bytes 1310720 | tf_op jit(solution)/shard_map/all_to_all | solution.py:13
  34.9 11.5 %collective-permute-start.3 = (f32[1,3,64,128]{3,2,1,0:T(8,128)S(1)}, f32[1,3,64,128]{3,2,1,0:T(8,128)S(1)}, u32[]{:S(2)}, u32[]{:S(2)}) collective-permute-start(f32[1,3,64,128]{3,2,1,0:T(8,128)S(1)} %get-tuple-element.18), channel_id=1, source_target_pairs={{0,64},{32,96},{64,0},{96,32},{1,65},{33,97},{65,1},{97,33},{2,66}... | collective-permute-start | bytes 294920 | tf_op jit(solution)/shard_map/ppermute | solution.py:56
  40.0 6.4 %collective-permute-start.5 = (f32[1,3,64,128]{3,2,1,0:T(8,128)S(1)}, f32[1,3,64,128]{3,2,1,0:T(8,128)S(1)}, u32[]{:S(2)}, u32[]{:S(2)}) collective-permute-start(f32[1,3,64,128]{3,2,1,0:T(8,128)S(1)} %get-tuple-element.19), channel_id=1, source_target_pairs={{0,96},{32,0},{64,32},{96,64},{1,97},{33,1},{65,33},{97,65},{2,98}... | collective-permute-start | bytes 294920 | tf_op jit(solution)/shard_map/ppermute | solution.py:56
  44.4 6.7 %collective-permute-start.4 = (f32[1,3,64,128]{3,2,1,0:T(8,128)S(1)}, f32[1,3,64,128]{3,2,1,0:T(8,128)S(1)}, u32[]{:S(2)}, u32[]{:S(2)}) collective-permute-start(f32[1,3,64,128]{3,2,1,0:T(8,128)S(1)} %get-tuple-element.20), channel_id=1, source_target_pairs={{0,32},{32,64},{64,96},{96,0},{1,33},{33,65},{65,97},{97,1},{2,34}... | collective-permute-start | bytes 294920 | tf_op jit(solution)/shard_map/ppermute | solution.py:56
  111.4 14.4 %all-to-all-start.5 = ((f32[16,8,512]{2,1,0:T(8,128)}), f32[16,8,512]{2,1,0:T(8,128)S(1)}, u32[]{:S(2)}, u32[]{:S(2)}) async-start(f32[16,8,512]{2,1,0:T(8,128)} %broadcast_in_dim.11), calls=%async_computation.5 | async-start | bytes 524288 | tf_op jit(solution)/shard_map/all_to_all | solution.py:13

commit v4 on v3

--- a/solution.py
+++ b/solution.py
@@ -3,7 +3,7 @@
 from jax import lax
 from jax.sharding import Mesh, PartitionSpec as P
 
-HIGH = lax.Precision.HIGH
+HIGH, HIGHEST = lax.Precision.HIGH, lax.Precision.HIGHEST
 ZL = ("zm", "zn")
 LANES = 128
 LATE = 3
@@ -44,15 +44,14 @@
 
     def product(got):
         field = got[:, :-i].reshape(nx, -1, i, j)
-        return jnp.einsum("xir,xuij->urj", got[:, -i:, :r], field, precision=HIGH)
+        return jnp.einsum("xir,xuij->urj", got[:, -i:, :r], field, precision=HIGHEST)
 
     products = product(got).reshape(nzl, -1, r, j)
-    products, came = lax.optimization_barrier((products, came))
     other = product(came).reshape(nx, -1, r, j)
 
     sums = exchange(products, ZL).sum(axis=0)
     tail = pick(other, me_x)[0]
-    for d in (2, 1, 3):
+    for d in (1, 3, 2):
         tail = tail + lax.ppermute(pick(other, (me_x + d) % nx), "x", [(x, (x + d) % nx) for x in range(nx)])[0]
     core = jnp.concatenate([sums, tail]).reshape(-1, j)
 
@@ -60,7 +59,7 @@
     gram = jnp.einsum("aj,yal->jyl", core, slices, precision=HIGH).reshape(j, ny * j)
     gram = gram * (1.0 / float(v * r * k * nzh * nc))
 
-    near, far = ("x", "c", "zn"), ("zm", "zh")
+    near, far = ("zn", "x", "c"), ("zm", "zh")
     count, others = nx * nc * nzl // 2, 2 * nzh
     part = exchange(gram.reshape(count, -1, ny * j), near).sum(axis=0)
     part = exchange(copies(part, others), far).sum(axis=0)

time: 127 us -> 128 us (level)
  waiting for transfers between devices: 19.1 us -> 17 us
  blocking collectives: 58.4 us -> 59.8 us
    ppermute x3, waiting for transfers between devices: 4.77 us -> 1.56 us  [local(): lax.ppermute(pick(other, (me_x + d) % nx), 'x', [(x, (x + d) % nx) for x...]
    all_to_all x3, blocking collectives: 58.4 us -> 59.8 us  [exchange(): return lax.all_to_all(a, axes, 0, 0)]
  transfers between devices with their start and end apart: 9 -> 9, of which waited for: 4 -> 5; matrix products, arithmetic and copies ran while one was open for 3% -> 3% of each run, Pallas kernels for 0% -> 0%
where the time goes in v4:
time: 128 us; the launch traced here: 127 us
  blocking collectives  59.8 us (47%)
  starting transfers between devices  39.6 us (31%)
  waiting for transfers between devices  17 us (13%)
  local copies, waits for them, and re-layouts  5.33 us (4%)
  matrix products  3.05 us (2%)
  other arithmetic  1.29 us (1%)
    all_to_all x3, blocking collectives, exchange(): return lax.all_to_all(a, axes, 0, 0)  59.8 us
    all_to_all x3, starting transfers between devices, exchange(): return lax.all_to_all(a, axes, 0, 0)  18.3 us
    ppermute x3, starting transfers between devices, local(): lax.ppermute(pick(other, (me_x + d) % nx), 'x', [(x, (x + d) % nx) for x...  11.4 us
    ppermute x3, starting transfers between devices, local(): lax.ppermute(pick(rest, (me_x + d) % nx), 'x', [(x, (x + d) % nx) for x i...  9.93 us
    ppermute x3, waiting for transfers between devices, local(): lax.ppermute(pick(rest, (me_x + d) % nx), 'x', [(x, (x + d) % nx) for x i...  8.05 us
    all_to_all x3, waiting for transfers between devices, exchange(): return lax.all_to_all(a, axes, 0, 0)  7.4 us
  transfers between devices with their start and end apart: 9, of which 5 were waited for; matrix products, arithmetic and copies ran while one was open for 3% of the time, Pallas kernels for 0%

profile of v4, /device:TPU:1, one launch (start us, length us, event | category | flops | bytes accessed | tf_op | source)
XLA Modules:
  0.0 127.0 jit_solution(6673736276060840590)
XLA Ops:
  0.6 1.5 %slice.24 = f32[4,4,1,32,3,128]{5,4,3,2,1,0:T(4,128)S(1)} slice(f32[4,4,2,32,4,128]{5,4,3,2,1,0:T(4,128)} %bitcast.55), slice={[0:4], [0:4], [1:2], [0:32], [1:4], [0:128]} | slice | bytes 1572864 | tf_op jit(solution)/shard_map/slice | solution.py:30
  2.9 1.0 pad_maximum_fusion.1
  3.9 6.4 %all-to-all-start.1 = ((f32[4,416,128]{2,1,0:T(8,128)}), f32[4,416,128]{2,1,0:T(8,128)S(1)}, u32[]{:S(2)}, u32[]{:S(2)}) async-start(f32[4,416,128]{2,1,0:T(8,128)} %pad_maximum_fusion.1), calls=%async_computation.1 | async-start | bytes 1703936 | tf_op jit(solution)/shard_map/all_to_all | solution.py:13
  10.8 3.1 %collective-permute-start = (f32[1,672,128]{2,1,0:T(8,128)S(1)}, f32[1,672,128]{2,1,0:T(8,128)S(1)}, u32[]{:S(2)}, u32[]{:S(2)}) collective-permute-start(f32[1,672,128]{2,1,0:T(8,128)S(1)} %get-tuple-element.11), channel_id=1, source_target_pairs={{0,32},{32,64},{64,96},{96,0},{1,33},{33,65},{65,97},{97,1},{2,34}... | collective-permute-start | bytes 1032200 | tf_op jit(solution)/shard_map/ppermute | solution.py:42
  13.9 3.4 %collective-permute-start.1 = (f32[1,672,128]{2,1,0:T(8,128)S(1)}, f32[1,672,128]{2,1,0:T(8,128)S(1)}, u32[]{:S(2)}, u32[]{:S(2)}) collective-permute-start(f32[1,672,128]{2,1,0:T(8,128)S(1)} %get-tuple-element.12), channel_id=1, source_target_pairs={{0,96},{32,0},{64,32},{96,64},{1,97},{33,1},{65,33},{97,65},{2,98}... | collective-permute-start | bytes 1032200 | tf_op jit(solution)/shard_map/ppermute | solution.py:42
  17.3 3.4 %collective-permute-start.2 = (f32[1,672,128]{2,1,0:T(8,128)S(1)}, f32[1,672,128]{2,1,0:T(8,128)S(1)}, u32[]{:S(2)}, u32[]{:S(2)}) collective-permute-start(f32[1,672,128]{2,1,0:T(8,128)S(1)} %get-tuple-element.13), channel_id=1, source_target_pairs={{0,64},{32,96},{64,0},{96,32},{1,65},{33,97},{65,1},{97,33},{2,66}... | collective-permute-start | bytes 1032200 | tf_op jit(solution)/shard_map/ppermute | solution.py:42
  20.8 1.8 %collective-permute-done.1 = f32[1,672,128]{2,1,0:T(8,128)S(1)} collective-permute-done((f32[1,672,128]{2,1,0:T(8,128)S(1)}, f32[1,672,128]{2,1,0:T(8,128)S(1)}, u32[]{:S(2)}, u32[]{:S(2)}) %collective-permute-start.1) | collective-permute-done | bytes 344096 | tf_op jit(solution)/shard_map/ppermute | solution.py:42
  22.6 6.2 %collective-permute-done.2 = f32[1,672,128]{2,1,0:T(8,128)S(1)} collective-permute-done((f32[1,672,128]{2,1,0:T(8,128)S(1)}, f32[1,672,128]{2,1,0:T(8,128)S(1)}, u32[]{:S(2)}, u32[]{:S(2)}) %collective-permute-start.2) | collective-permute-done | bytes 344096 | tf_op jit(solution)/shard_map/ppermute | solution.py:42
  29.0 1.7 %fusion.6 = f32[20,128,64,1]{1,2,0,3:T(8,128)} fusion(f32[4,20,32,128]{3,2,1,0:T(8,128)S(1)} %bitcast.53, f32[1,672,128]{2,1,0:T(8,128)S(1)} %collective-permute-done.2, f32[1,672,128]{2,1,0:T(8,128)S(1)} %collective-permute-done.1, f32[1,672,128]{2,1,0:T(8,128)S(1)} %collective-permute-done, f32[1,672,128]{2,1,0:T(8,128)S(1)} %get-tuple-element.10), kind=kOutput, calls=%fused_computation.22 | convolution fusion | flops 251682816 | bytes 3342336 | tf_op jit(solution)/shard_map/xir,xuij->urj/dot_general | solution.py:47
  30.8 4.1 %all-to-all-start = ((f32[4,5,64,128]{3,2,1,0:T(8,128)}), f32[4,5,64,128]{3,2,1,0:T(8,128)S(1)}, u32[]{:S(2)}, u32[]{:S(2)}) async-start(f32[4,5,64,128]{3,2,1,0:T(8,128)} %bitcast.13), calls=%async_computation | async-start | bytes 1310720 | tf_op jit(solution)/shard_map/all_to_all | solution.py:13
  35.5 5.2 %collective-permute-start.3 = (f32[1,3,64,128]{3,2,1,0:T(8,128)S(1)}, f32[1,3,64,128]{3,2,1,0:T(8,128)S(1)}, u32[]{:S(2)}, u32[]{:S(2)}) collective-permute-start(f32[1,3,64,128]{3,2,1,0:T(8,128)S(1)} %get-tuple-element.14), channel_id=1, source_target_pairs={{0,32},{32,64},{64,96},{96,0},{1,33},{33,65},{65,97},{97,1},{2,34}... | collective-permute-start | bytes 294920 | tf_op jit(solution)/shard_map/ppermute | solution.py:55
  40.8 3.6 %collective-permute-start.5 = (f32[1,3,64,128]{3,2,1,0:T(8,128)S(1)}, f32[1,3,64,128]{3,2,1,0:T(8,128)S(1)}, u32[]{:S(2)}, u32[]{:S(2)}) collective-permute-start(f32[1,3,64,128]{3,2,1,0:T(8,128)S(1)} %get-tuple-element.15), channel_id=1, source_target_pairs={{0,64},{32,96},{64,0},{96,32},{1,65},{33,97},{65,1},{97,33},{2,66}... | collective-permute-start | bytes 294920 | tf_op jit(solution)/shard_map/ppermute | solution.py:55
  44.3 2.6 %collective-permute-start.4 = (f32[1,3,64,128]{3,2,1,0:T(8,128)S(1)}, f32[1,3,64,128]{3,2,1,0:T(8,128)S(1)}, u32[]{:S(2)}, u32[]{:S(2)}) collective-permute-start(f32[1,3,64,128]{3,2,1,0:T(8,128)S(1)} %get-tuple-element.16), channel_id=1, source_target_pairs={{0,96},{32,0},{64,32},{96,64},{1,97},{33,1},{65,33},{97,65},{2,98}... | collective-permute-start | bytes 294920 | tf_op jit(solution)/shard_map/ppermute | solution.py:55
  47.0 1.1 all-to-all-done
  48.2 1.6 %collective-permute-done.4 = f32[1,3,64,128]{3,2,1,0:T(8,128)S(1)} collective-permute-done((f32[1,3,64,128]{3,2,1,0:T(8,128)S(1)}, f32[1,3,64,128]{3,2,1,0:T(8,128)S(1)}, u32[]{:S(2)}, u32[]{:S(2)}) %collective-permute-start.4) | collective-permute-done | bytes 98336 | tf_op jit(solution)/shard_map/ppermute | solution.py:55
  50.0 21.2 %all_to_all.30 = f32[4,512,128]{1,2,0:T(8,128)S(1)} all-to-all(f32[4,512,128]{1,2,0:T(8,128)S(1)} %broadcast_in_dim.9), channel_id=1, replica_groups=mesh['zm'=2,'zn'=2,'x'=4,'y'=4,'zh'=4,'c'=2] {'y'}, dimensions={0} | all-to-all | bytes 2097152 | tf_op jit(solution)/shard_map/all_to_all | solution.py:13
  71.2 0.7 fusion
  71.9 14.1 %all_to_all.31 = f32[16,8,512]{2,1,0:T(8,128)S(1)} all-to-all(f32[16,8,512]{2,1,0:T(8,128)S(1)} %fusion), channel_id=1, replica_groups=mesh['zm'=2,'zn'=2,'x'=4,'y'=4,'zh'=4,'c'=2] {'zn','x','c'}, dimensions={0} | all-to-all | bytes 524288 | tf_op jit(solution)/shard_map/all_to_all | solution.py:13
  86.0 24.6 %all_to_all.32 = f32[8,8,512]{2,1,0:T(8,128)S(1)} all-to-all(f32[8,8,512]{2,1,0:T(8,128)S(1)} %broadcast_in_dim.10), channel_id=1, replica_groups=mesh['zm'=2,'zn'=2,'x'=4,'y'=4,'zh'=4,'c'=2] {'zm','zh'}, dimensions={0} | all-to-all | bytes 262144 | tf_op jit(solution)/shard_map/all_to_all | solution.py:13
  110.6 0.7 broadcast_in_dim.11
  111.4 7.8 %all-to-all-start.5 = ((f32[16,8,512]{2,1,0:T(8,128)}), f32[16,8,512]{2,1,0:T(8,128)S(1)}, u32[]{:S(2)}, u32[]{:S(2)}) async-start(f32[16,8,512]{2,1,0:T(8,128)} %broadcast_in_dim.11), calls=%async_computation.5 | async-start | bytes 524288 | tf_op jit(solution)/shard_map/all_to_all | solution.py:13
  119.1 0.9 copy.17
  120.0 6.3 %all-to-all-done.5 = f32[16,8,512]{2,1,0:T(8,128)S(1)} async-done(((f32[16,8,512]{2,1,0:T(8,128)}), f32[16,8,512]{2,1,0:T(8,128)S(1)}, u32[]{:S(2)}, u32[]{:S(2)}) %all-to-all-start.5) | async-done | bytes 262176 | tf_op jit(solution)/shard_map/all_to_all | solution.py:13
  126.3 0.7 copy.24
  (27 shorter events, 2.4 us)
Async XLA Ops:
  2.1 0.7 copy-start.1
  2.9 7.4 %copy-start = (f32[32,32,4,128]{3,2,1,0:T(4,128)S(1)}, f32[32,32,4,128]{3,2,1,0:T(4,128)}, u32[]{:S(2)}) copy-start(f32[32,32,4,128]{3,2,1,0:T(4,128)} %param.2) | copy-start | bytes 6291460
  3.9 26.9 %all-to-all-start.1 = ((f32[4,416,128]{2,1,0:T(8,128)}), f32[4,416,128]{2,1,0:T(8,128)S(1)}, u32[]{:S(2)}, u32[]{:S(2)}) async-start(f32[4,416,128]{2,1,0:T(8,128)} %pad_maximum_fusion.1), calls=%async_computation.1 | async-start | bytes 1703936 | tf_op jit(solution)/shard_map/all_to_all | solution.py:13
  10.8 10.0 %collective-permute-start = (f32[1,672,128]{2,1,0:T(8,128)S(1)}, f32[1,672,128]{2,1,0:T(8,128)S(1)}, u32[]{:S(2)}, u32[]{:S(2)}) collective-permute-start(f32[1,672,128]{2,1,0:T(8,128)S(1)} %get-tuple-element.11), channel_id=1, source_target_pairs={{0,32},{32,64},{64,96},{96,0},{1,33},{33,65},{65,97},{97,1},{2,34}... | collective-permute-start | bytes 1032200 | tf_op jit(solution)/shard_map/ppermute | solution.py:42
  13.9 8.7 %collective-permute-start.1 = (f32[1,672,128]{2,1,0:T(8,128)S(1)}, f32[1,672,128]{2,1,0:T(8,128)S(1)}, u32[]{:S(2)}, u32[]{:S(2)}) collective-permute-start(f32[1,672,128]{2,1,0:T(8,128)S(1)} %get-tuple-element.12), channel_id=1, source_target_pairs={{0,96},{32,0},{64,32},{96,64},{1,97},{33,1},{65,33},{97,65},{2,98}... | collective-permute-start | bytes 1032200 | tf_op jit(solution)/shard_map/ppermute | solution.py:42
  17.3 11.5 %collective-permute-start.2 = (f32[1,672,128]{2,1,0:T(8,128)S(1)}, f32[1,672,128]{2,1,0:T(8,128)S(1)}, u32[]{:S(2)}, u32[]{:S(2)}) collective-permute-start(f32[1,672,128]{2,1,0:T(8,128)S(1)} %get-tuple-element.13), channel_id=1, source_target_pairs={{0,64},{32,96},{64,0},{96,32},{1,65},{33,97},{65,1},{97,33},{2,66}... | collective-permute-start | bytes 1032200 | tf_op jit(solution)/shard_map/ppermute | solution.py:42
  30.8 17.3 %all-to-all-start = ((f32[4,5,64,128]{3,2,1,0:T(8,128)}), f32[4,5,64,128]{3,2,1,0:T(8,128)S(1)}, u32[]{:S(2)}, u32[]{:S(2)}) async-start(f32[4,5,64,128]{3,2,1,0:T(8,128)} %bitcast.13), calls=%async_computation | async-start | bytes 1310720 | tf_op jit(solution)/shard_map/all_to_all | solution.py:13
  35.5 12.6 %collective-permute-start.3 = (f32[1,3,64,128]{3,2,1,0:T(8,128)S(1)}, f32[1,3,64,128]{3,2,1,0:T(8,128)S(1)}, u32[]{:S(2)}, u32[]{:S(2)}) collective-permute-start(f32[1,3,64,128]{3,2,1,0:T(8,128)S(1)} %get-tuple-element.14), channel_id=1, source_target_pairs={{0,32},{32,64},{64,96},{96,0},{1,33},{33,65},{65,97},{97,1},{2,34}... | collective-permute-start | bytes 294920 | tf_op jit(solution)/shard_map/ppermute | solution.py:55
  40.8 7.4 %collective-permute-start.5 = (f32[1,3,64,128]{3,2,1,0:T(8,128)S(1)}, f32[1,3,64,128]{3,2,1,0:T(8,128)S(1)}, u32[]{:S(2)}, u32[]{:S(2)}) collective-permute-start(f32[1,3,64,128]{3,2,1,0:T(8,128)S(1)} %get-tuple-element.15), channel_id=1, source_target_pairs={{0,64},{32,96},{64,0},{96,32},{1,65},{33,97},{65,1},{97,33},{2,66}... | collective-permute-start | bytes 294920 | tf_op jit(solution)/shard_map/ppermute | solution.py:55
  44.3 5.4 %collective-permute-start.4 = (f32[1,3,64,128]{3,2,1,0:T(8,128)S(1)}, f32[1,3,64,128]{3,2,1,0:T(8,128)S(1)}, u32[]{:S(2)}, u32[]{:S(2)}) collective-permute-start(f32[1,3,64,128]{3,2,1,0:T(8,128)S(1)} %get-tuple-element.16), channel_id=1, source_target_pairs={{0,96},{32,0},{64,32},{96,64},{1,97},{33,1},{65,33},{97,65},{2,98}... | collective-permute-start | bytes 294920 | tf_op jit(solution)/shard_map/ppermute | solution.py:55
  111.4 14.9 %all-to-all-start.5 = ((f32[16,8,512]{2,1,0:T(8,128)}), f32[16,8,512]{2,1,0:T(8,128)S(1)}, u32[]{:S(2)}, u32[]{:S(2)}) async-start(f32[16,8,512]{2,1,0:T(8,128)} %broadcast_in_dim.11), calls=%async_computation.5 | async-start | bytes 524288 | tf_op jit(solution)/shard_map/all_to_all | solution.py:13

commit v5 on v4

--- a/solution.py
+++ b/solution.py
@@ -40,13 +40,12 @@
     got = [pick(rest, me_x)]
     for d in (1, 3, 2):
         got.append(lax.ppermute(pick(rest, (me_x + d) % nx), "x", [(x, (x + d) % nx) for x in range(nx)]))
-    got = jnp.concatenate(got)
 
     def product(got):
-        field = got[:, :-i].reshape(nx, -1, i, j)
+        field = got[:, :-i].reshape(got.shape[0], -1, i, j)
         return jnp.einsum("xir,xuij->urj", got[:, -i:, :r], field, precision=HIGHEST)
 
-    products = product(got).reshape(nzl, -1, r, j)
+    products = (product(jnp.concatenate(got[:-1])) + product(got[-1])).reshape(nzl, -1, r, j)
     other = product(came).reshape(nx, -1, r, j)
 
     sums = exchange(products, ZL).sum(axis=0)

time: 128 us -> 128 us (level)
    dot_general x2 -> x3, matrix products: 2.32 us -> 2.95 us  [product(): jnp.einsum('xir,xuij->urj', got[:, -i:, :r], field, precision=HIGHEST)]
  transfers between devices with their start and end apart: 9 -> 9, of which waited for: 5 -> 5; matrix products, arithmetic and copies ran while one was open for 3% -> 4% of each run, Pallas kernels for 0% -> 0%
where the time goes in v5:
time: 128 us; the launch traced here: 127 us
  blocking collectives  59.3 us (46%)
  starting transfers between devices  39.6 us (31%)
  waiting for transfers between devices  17.1 us (13%)
  local copies, waits for them, and re-layouts  5.33 us (4%)
  matrix products  3.68 us (3%)
  other arithmetic  1.29 us (1%)
    all_to_all x3, blocking collectives, exchange(): return lax.all_to_all(a, axes, 0, 0)  59.3 us
    all_to_all x3, starting transfers between devices, exchange(): return lax.all_to_all(a, axes, 0, 0)  18.3 us
    ppermute x3, starting transfers between devices, local(): lax.ppermute(pick(other, (me_x + d) % nx), 'x', [(x, (x + d) % nx) for x...  11.4 us
    ppermute x3, starting transfers between devices, local(): lax.ppermute(pick(rest, (me_x + d) % nx), 'x', [(x, (x + d) % nx) for x i...  9.93 us
    ppermute x3, waiting for transfers between devices, local(): lax.ppermute(pick(rest, (me_x + d) % nx), 'x', [(x, (x + d) % nx) for x i...  7.87 us
    all_to_all x3, waiting for transfers between devices, exchange(): return lax.all_to_all(a, axes, 0, 0)  7.4 us
    dot_general x3, matrix products, product(): jnp.einsum('xir,xuij->urj', got[:, -i:, :r], field, precision=HIGHEST)  2.95 us
  transfers between devices with their start and end apart: 9, of which 5 were waited for; matrix products, arithmetic and copies ran while one was open for 4% of the time, Pallas kernels for 0%

profile of v5, /device:TPU:1, one launch (start us, length us, event | category | flops | bytes accessed | tf_op | source)
XLA Modules:
  0.0 127.3 jit_solution(11240217222887047010)
XLA Ops:
  0.6 1.5 %slice.32 = f32[4,4,1,32,3,128]{5,4,3,2,1,0:T(4,128)S(1)} slice(f32[4,4,2,32,4,128]{5,4,3,2,1,0:T(4,128)} %bitcast.62), slice={[0:4], [0:4], [1:2], [0:32], [1:4], [0:128]} | slice | bytes 1572864 | tf_op jit(solution)/shard_map/slice | solution.py:30
  2.9 1.0 pad_maximum_fusion.1
  3.9 6.4 %all-to-all-start.1 = ((f32[4,416,128]{2,1,0:T(8,128)}), f32[4,416,128]{2,1,0:T(8,128)S(1)}, u32[]{:S(2)}, u32[]{:S(2)}) async-start(f32[4,416,128]{2,1,0:T(8,128)} %pad_maximum_fusion.1), calls=%async_computation.1 | async-start | bytes 1703936 | tf_op jit(solution)/shard_map/all_to_all | solution.py:13
  10.8 3.1 %collective-permute-start = (f32[1,672,128]{2,1,0:T(8,128)S(1)}, f32[1,672,128]{2,1,0:T(8,128)S(1)}, u32[]{:S(2)}, u32[]{:S(2)}) collective-permute-start(f32[1,672,128]{2,1,0:T(8,128)S(1)} %get-tuple-element.11), channel_id=1, source_target_pairs={{0,32},{32,64},{64,96},{96,0},{1,33},{33,65},{65,97},{97,1},{2,34}... | collective-permute-start | bytes 1032200 | tf_op jit(solution)/shard_map/ppermute | solution.py:42
  13.9 3.4 %collective-permute-start.1 = (f32[1,672,128]{2,1,0:T(8,128)S(1)}, f32[1,672,128]{2,1,0:T(8,128)S(1)}, u32[]{:S(2)}, u32[]{:S(2)}) collective-permute-start(f32[1,672,128]{2,1,0:T(8,128)S(1)} %get-tuple-element.12), channel_id=1, source_target_pairs={{0,96},{32,0},{64,32},{96,64},{1,97},{33,1},{65,33},{97,65},{2,98}... | collective-permute-start | bytes 1032200 | tf_op jit(solution)/shard_map/ppermute | solution.py:42
  17.3 3.4 %collective-permute-start.2 = (f32[1,672,128]{2,1,0:T(8,128)S(1)}, f32[1,672,128]{2,1,0:T(8,128)S(1)}, u32[]{:S(2)}, u32[]{:S(2)}) collective-permute-start(f32[1,672,128]{2,1,0:T(8,128)S(1)} %get-tuple-element.13), channel_id=1, source_target_pairs={{0,64},{32,96},{64,0},{96,32},{1,65},{33,97},{65,1},{97,33},{2,66}... | collective-permute-start | bytes 1032200 | tf_op jit(solution)/shard_map/ppermute | solution.py:42
  20.8 1.8 %collective-permute-done.1 = f32[1,672,128]{2,1,0:T(8,128)S(1)} collective-permute-done((f32[1,672,128]{2,1,0:T(8,128)S(1)}, f32[1,672,128]{2,1,0:T(8,128)S(1)}, u32[]{:S(2)}, u32[]{:S(2)}) %collective-permute-start.1) | collective-permute-done | bytes 344096 | tf_op jit(solution)/shard_map/ppermute | solution.py:42
  22.8 6.1 %collective-permute-done.2 = f32[1,672,128]{2,1,0:T(8,128)S(1)} collective-permute-done((f32[1,672,128]{2,1,0:T(8,128)S(1)}, f32[1,672,128]{2,1,0:T(8,128)S(1)}, u32[]{:S(2)}, u32[]{:S(2)}) %collective-permute-start.2) | collective-permute-done | bytes 344096 | tf_op jit(solution)/shard_map/ppermute | solution.py:42
  28.9 0.7 fusion.11
  29.6 1.7 %fusion = f32[20,128,64]{1,2,0:T(8,128)} fusion(f32[20,128,64]{1,2,0:T(8,128)S(1)} %fusion.11, f32[3,20,32,128]{3,2,1,0:T(8,128)S(1)} %bitcast.68, f32[1,672,128]{2,1,0:T(8,128)S(1)} %collective-permute-done.1, f32[1,672,128]{2,1,0:T(8,128)S(1)} %collective-permute-done, f32[1,672,128]{2,1,0:T(8,128)S(1)} %get-tuple-element.10), kind=kOutput, calls=%fused_computation.5 | convolution fusion | flops 188919808 | bytes 3325952 | tf_op jit(solution)/shard_map/xir,xuij->urj/dot_general | solution.py:46
  31.2 4.1 %all-to-all-start = ((f32[4,5,64,128]{3,2,1,0:T(8,128)}), f32[4,5,64,128]{3,2,1,0:T(8,128)S(1)}, u32[]{:S(2)}, u32[]{:S(2)}) async-start(f32[4,5,64,128]{3,2,1,0:T(8,128)} %bitcast.16), calls=%async_computation | async-start | bytes 1310720 | tf_op jit(solution)/shard_map/all_to_all | solution.py:13
  36.0 5.2 %collective-permute-start.3 = (f32[1,3,64,128]{3,2,1,0:T(8,128)S(1)}, f32[1,3,64,128]{3,2,1,0:T(8,128)S(1)}, u32[]{:S(2)}, u32[]{:S(2)}) collective-permute-start(f32[1,3,64,128]{3,2,1,0:T(8,128)S(1)} %get-tuple-element.14), channel_id=1, source_target_pairs={{0,32},{32,64},{64,96},{96,0},{1,33},{33,65},{65,97},{97,1},{2,34}... | collective-permute-start | bytes 294920 | tf_op jit(solution)/shard_map/ppermute | solution.py:54
  41.2 3.6 %collective-permute-start.5 = (f32[1,3,64,128]{3,2,1,0:T(8,128)S(1)}, f32[1,3,64,128]{3,2,1,0:T(8,128)S(1)}, u32[]{:S(2)}, u32[]{:S(2)}) collective-permute-start(f32[1,3,64,128]{3,2,1,0:T(8,128)S(1)} %get-tuple-element.15), channel_id=1, source_target_pairs={{0,64},{32,96},{64,0},{96,32},{1,65},{33,97},{65,1},{97,33},{2,66}... | collective-permute-start | bytes 294920 | tf_op jit(solution)/shard_map/ppermute | solution.py:54
  44.8 2.6 %collective-permute-start.4 = (f32[1,3,64,128]{3,2,1,0:T(8,128)S(1)}, f32[1,3,64,128]{3,2,1,0:T(8,128)S(1)}, u32[]{:S(2)}, u32[]{:S(2)}) collective-permute-start(f32[1,3,64,128]{3,2,1,0:T(8,128)S(1)} %get-tuple-element.16), channel_id=1, source_target_pairs={{0,96},{32,0},{64,32},{96,64},{1,97},{33,1},{65,33},{97,65},{2,98}... | collective-permute-start | bytes 294920 | tf_op jit(solution)/shard_map/ppermute | solution.py:54
  47.5 1.1 all-to-all-done
  48.6 1.8 %collective-permute-done.4 = f32[1,3,64,128]{3,2,1,0:T(8,128)S(1)} collective-permute-done((f32[1,3,64,128]{3,2,1,0:T(8,128)S(1)}, f32[1,3,64,128]{3,2,1,0:T(8,128)S(1)}, u32[]{:S(2)}, u32[]{:S(2)}) %collective-permute-start.4) | collective-permute-done | bytes 98336 | tf_op jit(solution)/shard_map/ppermute | solution.py:54
  50.8 20.6 %all_to_all.30 = f32[4,512,128]{1,2,0:T(8,128)S(1)} all-to-all(f32[4,512,128]{1,2,0:T(8,128)S(1)} %broadcast_in_dim.9), channel_id=1, replica_groups=mesh['zm'=2,'zn'=2,'x'=4,'y'=4,'zh'=4,'c'=2] {'y'}, dimensions={0} | all-to-all | bytes 2097152 | tf_op jit(solution)/shard_map/all_to_all | solution.py:13
  71.4 0.7 fusion.1
  72.1 14.2 %all_to_all.31 = f32[16,8,512]{2,1,0:T(8,128)S(1)} all-to-all(f32[16,8,512]{2,1,0:T(8,128)S(1)} %fusion.1), channel_id=1, replica_groups=mesh['zm'=2,'zn'=2,'x'=4,'y'=4,'zh'=4,'c'=2] {'zn','x','c'}, dimensions={0} | all-to-all | bytes 524288 | tf_op jit(solution)/shard_map/all_to_all | solution.py:13
  86.3 24.6 %all_to_all.32 = f32[8,8,512]{2,1,0:T(8,128)S(1)} all-to-all(f32[8,8,512]{2,1,0:T(8,128)S(1)} %broadcast_in_dim.10), channel_id=1, replica_groups=mesh['zm'=2,'zn'=2,'x'=4,'y'=4,'zh'=4,'c'=2] {'zm','zh'}, dimensions={0} | all-to-all | bytes 262144 | tf_op jit(solution)/shard_map/all_to_all | solution.py:13
  110.9 0.7 broadcast_in_dim.11
  111.6 7.8 %all-to-all-start.5 = ((f32[16,8,512]{2,1,0:T(8,128)}), f32[16,8,512]{2,1,0:T(8,128)S(1)}, u32[]{:S(2)}, u32[]{:S(2)}) async-start(f32[16,8,512]{2,1,0:T(8,128)} %broadcast_in_dim.11), calls=%async_computation.5 | async-start | bytes 524288 | tf_op jit(solution)/shard_map/all_to_all | solution.py:13
  119.4 0.9 copy.17
  120.3 6.3 %all-to-all-done.5 = f32[16,8,512]{2,1,0:T(8,128)S(1)} async-done(((f32[16,8,512]{2,1,0:T(8,128)}), f32[16,8,512]{2,1,0:T(8,128)S(1)}, u32[]{:S(2)}, u32[]{:S(2)}) %all-to-all-start.5) | async-done | bytes 262176 | tf_op jit(solution)/shard_map/all_to_all | solution.py:13
  (29 shorter events, 3.1 us)
Async XLA Ops:
  2.1 0.7 copy-start.1
  2.9 7.4 %copy-start = (f32[32,32,4,128]{3,2,1,0:T(4,128)S(1)}, f32[32,32,4,128]{3,2,1,0:T(4,128)}, u32[]{:S(2)}) copy-start(f32[32,32,4,128]{3,2,1,0:T(4,128)} %param.2) | copy-start | bytes 6291460
  3.9 27.4 %all-to-all-start.1 = ((f32[4,416,128]{2,1,0:T(8,128)}), f32[4,416,128]{2,1,0:T(8,128)S(1)}, u32[]{:S(2)}, u32[]{:S(2)}) async-start(f32[4,416,128]{2,1,0:T(8,128)} %pad_maximum_fusion.1), calls=%async_computation.1 | async-start | bytes 1703936 | tf_op jit(solution)/shard_map/all_to_all | solution.py:13
  10.8 10.0 %collective-permute-start = (f32[1,672,128]{2,1,0:T(8,128)S(1)}, f32[1,672,128]{2,1,0:T(8,128)S(1)}, u32[]{:S(2)}, u32[]{:S(2)}) collective-permute-start(f32[1,672,128]{2,1,0:T(8,128)S(1)} %get-tuple-element.11), channel_id=1, source_target_pairs={{0,32},{32,64},{64,96},{96,0},{1,33},{33,65},{65,97},{97,1},{2,34}... | collective-permute-start | bytes 1032200 | tf_op jit(solution)/shard_map/ppermute | solution.py:42
  13.9 8.7 %collective-permute-start.1 = (f32[1,672,128]{2,1,0:T(8,128)S(1)}, f32[1,672,128]{2,1,0:T(8,128)S(1)}, u32[]{:S(2)}, u32[]{:S(2)}) collective-permute-start(f32[1,672,128]{2,1,0:T(8,128)S(1)} %get-tuple-element.12), channel_id=1, source_target_pairs={{0,96},{32,0},{64,32},{96,64},{1,97},{33,1},{65,33},{97,65},{2,98}... | collective-permute-start | bytes 1032200 | tf_op jit(solution)/shard_map/ppermute | solution.py:42
  17.3 11.5 %collective-permute-start.2 = (f32[1,672,128]{2,1,0:T(8,128)S(1)}, f32[1,672,128]{2,1,0:T(8,128)S(1)}, u32[]{:S(2)}, u32[]{:S(2)}) collective-permute-start(f32[1,672,128]{2,1,0:T(8,128)S(1)} %get-tuple-element.13), channel_id=1, source_target_pairs={{0,64},{32,96},{64,0},{96,32},{1,65},{33,97},{65,1},{97,33},{2,66}... | collective-permute-start | bytes 1032200 | tf_op jit(solution)/shard_map/ppermute | solution.py:42
  31.2 17.3 %all-to-all-start = ((f32[4,5,64,128]{3,2,1,0:T(8,128)}), f32[4,5,64,128]{3,2,1,0:T(8,128)S(1)}, u32[]{:S(2)}, u32[]{:S(2)}) async-start(f32[4,5,64,128]{3,2,1,0:T(8,128)} %bitcast.16), calls=%async_computation | async-start | bytes 1310720 | tf_op jit(solution)/shard_map/all_to_all | solution.py:13
  36.0 12.6 %collective-permute-start.3 = (f32[1,3,64,128]{3,2,1,0:T(8,128)S(1)}, f32[1,3,64,128]{3,2,1,0:T(8,128)S(1)}, u32[]{:S(2)}, u32[]{:S(2)}) collective-permute-start(f32[1,3,64,128]{3,2,1,0:T(8,128)S(1)} %get-tuple-element.14), channel_id=1, source_target_pairs={{0,32},{32,64},{64,96},{96,0},{1,33},{33,65},{65,97},{97,1},{2,34}... | collective-permute-start | bytes 294920 | tf_op jit(solution)/shard_map/ppermute | solution.py:54
  41.2 7.4 %collective-permute-start.5 = (f32[1,3,64,128]{3,2,1,0:T(8,128)S(1)}, f32[1,3,64,128]{3,2,1,0:T(8,128)S(1)}, u32[]{:S(2)}, u32[]{:S(2)}) collective-permute-start(f32[1,3,64,128]{3,2,1,0:T(8,128)S(1)} %get-tuple-element.15), channel_id=1, source_target_pairs={{0,64},{32,96},{64,0},{96,32},{1,65},{33,97},{65,1},{97,33},{2,66}... | collective-permute-start | bytes 294920 | tf_op jit(solution)/shard_map/ppermute | solution.py:54
  44.8 5.7 %collective-permute-start.4 = (f32[1,3,64,128]{3,2,1,0:T(8,128)S(1)}, f32[1,3,64,128]{3,2,1,0:T(8,128)S(1)}, u32[]{:S(2)}, u32[]{:S(2)}) collective-permute-start(f32[1,3,64,128]{3,2,1,0:T(8,128)S(1)} %get-tuple-element.16), channel_id=1, source_target_pairs={{0,96},{32,0},{64,32},{96,64},{1,97},{33,1},{65,33},{97,65},{2,98}... | collective-permute-start | bytes 294920 | tf_op jit(solution)/shard_map/ppermute | solution.py:54
  111.6 14.9 %all-to-all-start.5 = ((f32[16,8,512]{2,1,0:T(8,128)}), f32[16,8,512]{2,1,0:T(8,128)S(1)}, u32[]{:S(2)}, u32[]{:S(2)}) async-start(f32[16,8,512]{2,1,0:T(8,128)} %broadcast_in_dim.11), calls=%async_computation.5 | async-start | bytes 524288 | tf_op jit(solution)/shard_map/all_to_all | solution.py:13

commit v6 on v5

--- a/solution.py
+++ b/solution.py
@@ -45,7 +45,8 @@
         field = got[:, :-i].reshape(got.shape[0], -1, i, j)
         return jnp.einsum("xir,xuij->urj", got[:, -i:, :r], field, precision=HIGHEST)
 
-    products = (product(jnp.concatenate(got[:-1])) + product(got[-1])).reshape(nzl, -1, r, j)
+    products, last = lax.optimization_barrier((product(jnp.concatenate(got[:-1])), got[-1]))
+    products = (products + product(last)).reshape(nzl, -1, r, j)
     other = product(came).reshape(nx, -1, r, j)
 
     sums = exchange(products, ZL).sum(axis=0)

time: 128 us -> 127 us (level)
  no operation moved by 1% of the time
where the time goes in v6:
time: 127 us; the launch traced here: 126 us
  blocking collectives  59.2 us (47%)
  starting transfers between devices  39.6 us (31%)
  waiting for transfers between devices  16.3 us (13%)
  local copies, waits for them, and re-layouts  5.33 us (4%)
  matrix products  2.82 us (2%)
  other arithmetic  2.23 us (2%)
    all_to_all x3, blocking collectives, exchange(): return lax.all_to_all(a, axes, 0, 0)  59.2 us
    all_to_all x3, starting transfers between devices, exchange(): return lax.all_to_all(a, axes, 0, 0)  18.3 us
    ppermute x3, starting transfers between devices, local(): lax.ppermute(pick(other, (me_x + d) % nx), 'x', [(x, (x + d) % nx) for x...  11.4 us
    ppermute x3, starting transfers between devices, local(): lax.ppermute(pick(rest, (me_x + d) % nx), 'x', [(x, (x + d) % nx) for x i...  9.93 us
    ppermute x3, waiting for transfers between devices, local(): lax.ppermute(pick(rest, (me_x + d) % nx), 'x', [(x, (x + d) % nx) for x i...  7.05 us
    all_to_all x3, waiting for transfers between devices, exchange(): return lax.all_to_all(a, axes, 0, 0)  6.3 us
    ppermute x3, waiting for transfers between devices, local(): lax.ppermute(pick(other, (me_x + d) % nx), 'x', [(x, (x + d) % nx) for x...  2.94 us
  transfers between devices with their start and end apart: 9, of which 5 were waited for; matrix products, arithmetic and copies ran while one was open for 4% of the time, Pallas kernels for 0%

profile of v6, /device:TPU:1, one launch (start us, length us, event | category | flops | bytes accessed | tf_op | source)
XLA Modules:
  0.0 126.4 jit_solution(15111260555048170246)
XLA Ops:
  0.6 1.5 %slice.32 = f32[4,4,1,32,3,128]{5,4,3,2,1,0:T(4,128)S(1)} slice(f32[4,4,2,32,4,128]{5,4,3,2,1,0:T(4,128)} %bitcast.62), slice={[0:4], [0:4], [1:2], [0:32], [1:4], [0:128]} | slice | bytes 1572864 | tf_op jit(solution)/shard_map/slice | solution.py:30
  2.9 1.0 pad_maximum_fusion.1
  3.9 6.4 %all-to-all-start.1 = ((f32[4,416,128]{2,1,0:T(8,128)}), f32[4,416,128]{2,1,0:T(8,128)S(1)}, u32[]{:S(2)}, u32[]{:S(2)}) async-start(f32[4,416,128]{2,1,0:T(8,128)} %pad_maximum_fusion.1), calls=%async_computation.1 | async-start | bytes 1703936 | tf_op jit(solution)/shard_map/all_to_all | solution.py:13
  10.8 3.1 %collective-permute-start = (f32[1,672,128]{2,1,0:T(8,128)S(1)}, f32[1,672,128]{2,1,0:T(8,128)S(1)}, u32[]{:S(2)}, u32[]{:S(2)}) collective-permute-start(f32[1,672,128]{2,1,0:T(8,128)S(1)} %get-tuple-element.16), channel_id=1, source_target_pairs={{0,32},{32,64},{64,96},{96,0},{1,33},{33,65},{65,97},{97,1},{2,34}... | collective-permute-start | bytes 1032200 | tf_op jit(solution)/shard_map/ppermute | solution.py:42
  13.9 3.4 %collective-permute-start.1 = (f32[1,672,128]{2,1,0:T(8,128)S(1)}, f32[1,672,128]{2,1,0:T(8,128)S(1)}, u32[]{:S(2)}, u32[]{:S(2)}) collective-permute-start(f32[1,672,128]{2,1,0:T(8,128)S(1)} %get-tuple-element.17), channel_id=1, source_target_pairs={{0,96},{32,0},{64,32},{96,64},{1,97},{33,1},{65,33},{97,65},{2,98}... | collective-permute-start | bytes 1032200 | tf_op jit(solution)/shard_map/ppermute | solution.py:42
  17.3 3.4 %collective-permute-start.2 = (f32[1,672,128]{2,1,0:T(8,128)S(1)}, f32[1,672,128]{2,1,0:T(8,128)S(1)}, u32[]{:S(2)}, u32[]{:S(2)}) collective-permute-start(f32[1,672,128]{2,1,0:T(8,128)S(1)} %get-tuple-element.14), channel_id=1, source_target_pairs={{0,64},{32,96},{64,0},{96,32},{1,65},{33,97},{65,1},{97,33},{2,66}... | collective-permute-start | bytes 1032200 | tf_op jit(solution)/shard_map/ppermute | solution.py:42
  20.8 1.8 %collective-permute-done.1 = f32[1,672,128]{2,1,0:T(8,128)S(1)} collective-permute-done((f32[1,672,128]{2,1,0:T(8,128)S(1)}, f32[1,672,128]{2,1,0:T(8,128)S(1)}, u32[]{:S(2)}, u32[]{:S(2)}) %collective-permute-start.1) | collective-permute-done | bytes 344096 | tf_op jit(solution)/shard_map/ppermute | solution.py:42
  22.8 0.8 convolution_bitcast_fusion
  23.6 5.2 %collective-permute-done.2 = f32[1,672,128]{2,1,0:T(8,128)S(1)} collective-permute-done((f32[1,672,128]{2,1,0:T(8,128)S(1)}, f32[1,672,128]{2,1,0:T(8,128)S(1)}, u32[]{:S(2)}, u32[]{:S(2)}) %collective-permute-start.2) | collective-permute-done | bytes 344096 | tf_op jit(solution)/shard_map/ppermute | solution.py:42
  28.9 0.7 convolution_bitcast_fusion.1
  29.6 0.9 add.72
  30.5 4.1 %all-to-all-start = ((f32[4,5,64,128]{3,2,1,0:T(8,128)}), f32[4,5,64,128]{3,2,1,0:T(8,128)S(1)}, u32[]{:S(2)}, u32[]{:S(2)}) async-start(f32[4,5,64,128]{3,2,1,0:T(8,128)} %bitcast.17), calls=%async_computation | async-start | bytes 1310720 | tf_op jit(solution)/shard_map/all_to_all | solution.py:13
  35.3 5.2 %collective-permute-start.3 = (f32[1,3,64,128]{3,2,1,0:T(8,128)S(1)}, f32[1,3,64,128]{3,2,1,0:T(8,128)S(1)}, u32[]{:S(2)}, u32[]{:S(2)}) collective-permute-start(f32[1,3,64,128]{3,2,1,0:T(8,128)S(1)} %get-tuple-element.18), channel_id=1, source_target_pairs={{0,32},{32,64},{64,96},{96,0},{1,33},{33,65},{65,97},{97,1},{2,34}... | collective-permute-start | bytes 294920 | tf_op jit(solution)/shard_map/ppermute | solution.py:55
  40.5 3.6 %collective-permute-start.5 = (f32[1,3,64,128]{3,2,1,0:T(8,128)S(1)}, f32[1,3,64,128]{3,2,1,0:T(8,128)S(1)}, u32[]{:S(2)}, u32[]{:S(2)}) collective-permute-start(f32[1,3,64,128]{3,2,1,0:T(8,128)S(1)} %get-tuple-element.19), channel_id=1, source_target_pairs={{0,64},{32,96},{64,0},{96,32},{1,65},{33,97},{65,1},{97,33},{2,66}... | collective-permute-start | bytes 294920 | tf_op jit(solution)/shard_map/ppermute | solution.py:55
  44.1 2.6 %collective-permute-start.4 = (f32[1,3,64,128]{3,2,1,0:T(8,128)S(1)}, f32[1,3,64,128]{3,2,1,0:T(8,128)S(1)}, u32[]{:S(2)}, u32[]{:S(2)}) collective-permute-start(f32[1,3,64,128]{3,2,1,0:T(8,128)S(1)} %get-tuple-element.20), channel_id=1, source_target_pairs={{0,96},{32,0},{64,32},{96,64},{1,97},{33,1},{65,33},{97,65},{2,98}... | collective-permute-start | bytes 294920 | tf_op jit(solution)/shard_map/ppermute | solution.py:55
  47.5 2.2 %collective-permute-done.4 = f32[1,3,64,128]{3,2,1,0:T(8,128)S(1)} collective-permute-done((f32[1,3,64,128]{3,2,1,0:T(8,128)S(1)}, f32[1,3,64,128]{3,2,1,0:T(8,128)S(1)}, u32[]{:S(2)}, u32[]{:S(2)}) %collective-permute-start.4) | collective-permute-done | bytes 98336 | tf_op jit(solution)/shard_map/ppermute | solution.py:55
  50.1 17.5 %all_to_all.30 = f32[4,512,128]{1,2,0:T(8,128)S(1)} all-to-all(f32[4,512,128]{1,2,0:T(8,128)S(1)} %broadcast_in_dim.9), channel_id=1, replica_groups=mesh['zm'=2,'zn'=2,'x'=4,'y'=4,'zh'=4,'c'=2] {'y'}, dimensions={0} | all-to-all | bytes 2097152 | tf_op jit(solution)/shard_map/all_to_all | solution.py:13
  67.6 0.7 fusion
  68.3 17.1 %all_to_all.31 = f32[16,8,512]{2,1,0:T(8,128)S(1)} all-to-all(f32[16,8,512]{2,1,0:T(8,128)S(1)} %fusion), channel_id=1, replica_groups=mesh['zm'=2,'zn'=2,'x'=4,'y'=4,'zh'=4,'c'=2] {'zn','x','c'}, dimensions={0} | all-to-all | bytes 524288 | tf_op jit(solution)/shard_map/all_to_all | solution.py:13
  85.4 24.6 %all_to_all.32 = f32[8,8,512]{2,1,0:T(8,128)S(1)} all-to-all(f32[8,8,512]{2,1,0:T(8,128)S(1)} %broadcast_in_dim.10), channel_id=1, replica_groups=mesh['zm'=2,'zn'=2,'x'=4,'y'=4,'zh'=4,'c'=2] {'zm','zh'}, dimensions={0} | all-to-all | bytes 262144 | tf_op jit(solution)/shard_map/all_to_all | solution.py:13
  110.0 0.7 broadcast_in_dim.11
  110.7 7.8 %all-to-all-start.5 = ((f32[16,8,512]{2,1,0:T(8,128)}), f32[16,8,512]{2,1,0:T(8,128)S(1)}, u32[]{:S(2)}, u32[]{:S(2)}) async-start(f32[16,8,512]{2,1,0:T(8,128)} %broadcast_in_dim.11), calls=%async_computation.5 | async-start | bytes 524288 | tf_op jit(solution)/shard_map/all_to_all | solution.py:13
  118.5 0.9 copy.17
  119.4 6.3 %all-to-all-done.5 = f32[16,8,512]{2,1,0:T(8,128)S(1)} async-done(((f32[16,8,512]{2,1,0:T(8,128)}), f32[16,8,512]{2,1,0:T(8,128)S(1)}, u32[]{:S(2)}, u32[]{:S(2)}) %all-to-all-start.5) | async-done | bytes 262176 | tf_op jit(solution)/shard_map/all_to_all | solution.py:13
  (30 shorter events, 3.8 us)
Async XLA Ops:
  2.1 0.7 copy-start.1
  2.9 7.4 %copy-start = (f32[32,32,4,128]{3,2,1,0:T(4,128)S(1)}, f32[32,32,4,128]{3,2,1,0:T(4,128)}, u32[]{:S(2)}) copy-start(f32[32,32,4,128]{3,2,1,0:T(4,128)} %param.2) | copy-start | bytes 6291460
  3.9 26.7 %all-to-all-start.1 = ((f32[4,416,128]{2,1,0:T(8,128)}), f32[4,416,128]{2,1,0:T(8,128)S(1)}, u32[]{:S(2)}, u32[]{:S(2)}) async-start(f32[4,416,128]{2,1,0:T(8,128)} %pad_maximum_fusion.1), calls=%async_computation.1 | async-start | bytes 1703936 | tf_op jit(solution)/shard_map/all_to_all | solution.py:13
  10.8 10.0 %collective-permute-start = (f32[1,672,128]{2,1,0:T(8,128)S(1)}, f32[1,672,128]{2,1,0:T(8,128)S(1)}, u32[]{:S(2)}, u32[]{:S(2)}) collective-permute-start(f32[1,672,128]{2,1,0:T(8,128)S(1)} %get-tuple-element.16), channel_id=1, source_target_pairs={{0,32},{32,64},{64,96},{96,0},{1,33},{33,65},{65,97},{97,1},{2,34}... | collective-permute-start | bytes 1032200 | tf_op jit(solution)/shard_map/ppermute | solution.py:42
  13.9 8.7 %collective-permute-start.1 = (f32[1,672,128]{2,1,0:T(8,128)S(1)}, f32[1,672,128]{2,1,0:T(8,128)S(1)}, u32[]{:S(2)}, u32[]{:S(2)}) collective-permute-start(f32[1,672,128]{2,1,0:T(8,128)S(1)} %get-tuple-element.17), channel_id=1, source_target_pairs={{0,96},{32,0},{64,32},{96,64},{1,97},{33,1},{65,33},{97,65},{2,98}... | collective-permute-start | bytes 1032200 | tf_op jit(solution)/shard_map/ppermute | solution.py:42
  17.3 11.5 %collective-permute-start.2 = (f32[1,672,128]{2,1,0:T(8,128)S(1)}, f32[1,672,128]{2,1,0:T(8,128)S(1)}, u32[]{:S(2)}, u32[]{:S(2)}) collective-permute-start(f32[1,672,128]{2,1,0:T(8,128)S(1)} %get-tuple-element.14), channel_id=1, source_target_pairs={{0,64},{32,96},{64,0},{96,32},{1,65},{33,97},{65,1},{97,33},{2,66}... | collective-permute-start | bytes 1032200 | tf_op jit(solution)/shard_map/ppermute | solution.py:42
  30.5 16.2 %all-to-all-start = ((f32[4,5,64,128]{3,2,1,0:T(8,128)}), f32[4,5,64,128]{3,2,1,0:T(8,128)S(1)}, u32[]{:S(2)}, u32[]{:S(2)}) async-start(f32[4,5,64,128]{3,2,1,0:T(8,128)} %bitcast.17), calls=%async_computation | async-start | bytes 1310720 | tf_op jit(solution)/shard_map/all_to_all | solution.py:13
  35.3 11.5 %collective-permute-start.3 = (f32[1,3,64,128]{3,2,1,0:T(8,128)S(1)}, f32[1,3,64,128]{3,2,1,0:T(8,128)S(1)}, u32[]{:S(2)}, u32[]{:S(2)}) collective-permute-start(f32[1,3,64,128]{3,2,1,0:T(8,128)S(1)} %get-tuple-element.18), channel_id=1, source_target_pairs={{0,32},{32,64},{64,96},{96,0},{1,33},{33,65},{65,97},{97,1},{2,34}... | collective-permute-start | bytes 294920 | tf_op jit(solution)/shard_map/ppermute | solution.py:55
  40.5 7.0 %collective-permute-start.5 = (f32[1,3,64,128]{3,2,1,0:T(8,128)S(1)}, f32[1,3,64,128]{3,2,1,0:T(8,128)S(1)}, u32[]{:S(2)}, u32[]{:S(2)}) collective-permute-start(f32[1,3,64,128]{3,2,1,0:T(8,128)S(1)} %get-tuple-element.19), channel_id=1, source_target_pairs={{0,64},{32,96},{64,0},{96,32},{1,65},{33,97},{65,1},{97,33},{2,66}... | collective-permute-start | bytes 294920 | tf_op jit(solution)/shard_map/ppermute | solution.py:55
  44.1 5.7 %collective-permute-start.4 = (f32[1,3,64,128]{3,2,1,0:T(8,128)S(1)}, f32[1,3,64,128]{3,2,1,0:T(8,128)S(1)}, u32[]{:S(2)}, u32[]{:S(2)}) collective-permute-start(f32[1,3,64,128]{3,2,1,0:T(8,128)S(1)} %get-tuple-element.20), channel_id=1, source_target_pairs={{0,96},{32,0},{64,32},{96,64},{1,97},{33,1},{65,33},{97,65},{2,98}... | collective-permute-start | bytes 294920 | tf_op jit(solution)/shard_map/ppermute | solution.py:55
  110.7 14.9 %all-to-all-start.5 = ((f32[16,8,512]{2,1,0:T(8,128)}), f32[16,8,512]{2,1,0:T(8,128)S(1)}, u32[]{:S(2)}, u32[]{:S(2)}) async-start(f32[16,8,512]{2,1,0:T(8,128)} %broadcast_in_dim.11), calls=%async_computation.5 | async-start | bytes 524288 | tf_op jit(solution)/shard_map/all_to_all | solution.py:13

commit v7 on v6

--- a/solution.py
+++ b/solution.py
@@ -5,7 +5,6 @@
 
 HIGH, HIGHEST = lax.Precision.HIGH, lax.Precision.HIGHEST
 ZL = ("zm", "zn")
-LANES = 128
 LATE = 3
 
 
@@ -30,7 +29,7 @@
     late = tensor.reshape(nzl, nx, mine, i, k, j)[:, :, 1, :, k - LATE :].swapaxes(2, 3)
     late, tensor = lax.optimization_barrier((late, tensor))
     slabs = tensor.reshape(nzl, nx, mine, i, k, j).swapaxes(3, 4).reshape(nzl, nx, mine * k, i, j)
-    factor = jnp.pad(factor, ((0, 0), (0, LANES - r)))
+    factor = jnp.concatenate([factor[: i // 2], factor[i // 2 :]], axis=1)
 
     late = late.reshape(nzl, -1, j)
     late = jnp.concatenate([late, copies(factor, nzl)], axis=1)
@@ -42,8 +41,9 @@
         got.append(lax.ppermute(pick(rest, (me_x + d) % nx), "x", [(x, (x + d) % nx) for x in range(nx)]))
 
     def product(got):
-        field = got[:, :-i].reshape(got.shape[0], -1, i, j)
-        return jnp.einsum("xir,xuij->urj", got[:, -i:, :r], field, precision=HIGHEST)
+        field = got[:, : -i // 2].reshape(got.shape[0], -1, i, j)
+        rows_of = jnp.concatenate([got[:, -i // 2 :, :r], got[:, -i // 2 :, r:]], axis=1)
+        return jnp.einsum("xir,xuij->urj", rows_of, field, precision=HIGHEST)
 
     products, last = lax.optimization_barrier((product(jnp.concatenate(got[:-1])), got[-1]))
     products = (products + product(last)).reshape(nzl, -1, r, j)

time: 127 us -> 127 us (level)
  no operation moved by 1% of the time
where the time goes in v7:
time: 127 us; the launch traced here: 126 us
  blocking collectives  59 us (46%)
  starting transfers between devices  40 us (31%)
  waiting for transfers between devices  15.6 us (12%)
  local copies, waits for them, and re-layouts  5.56 us (4%)
  matrix products  2.89 us (2%)
  other arithmetic  2.28 us (2%)
    all_to_all x3, blocking collectives, exchange(): return lax.all_to_all(a, axes, 0, 0)  59 us
    all_to_all x3, starting transfers between devices, exchange(): return lax.all_to_all(a, axes, 0, 0)  18.8 us
    ppermute x3, starting transfers between devices, local(): lax.ppermute(pick(other, (me_x + d) % nx), 'x', [(x, (x + d) % nx) for x...  11.3 us
    ppermute x3, starting transfers between devices, local(): lax.ppermute(pick(rest, (me_x + d) % nx), 'x', [(x, (x + d) % nx) for x i...  9.93 us
    ppermute x3, waiting for transfers between devices, local(): lax.ppermute(pick(rest, (me_x + d) % nx), 'x', [(x, (x + d) % nx) for x i...  6.31 us
    all_to_all x3, waiting for transfers between devices, exchange(): return lax.all_to_all(a, axes, 0, 0)  6.3 us
    ppermute x3, waiting for transfers between devices, local(): lax.ppermute(pick(other, (me_x + d) % nx), 'x', [(x, (x + d) % nx) for x...  3.01 us
  transfers between devices with their start and end apart: 9, of which 5 were waited for; matrix products, arithmetic and copies ran while one was open for 4% of the time, Pallas kernels for 0%

profile of v7, /device:TPU:1, one launch (start us, length us, event | category | flops | bytes accessed | tf_op | source)
XLA Modules:
  0.0 126.3 jit_solution(12726918337651252371)
XLA Ops:
  1.3 1.5 %slice.52 = f32[4,4,1,32,3,128]{5,4,3,2,1,0:T(4,128)S(1)} slice(f32[4,4,2,32,4,128]{5,4,3,2,1,0:T(4,128)} %bitcast.62), slice={[0:4], [0:4], [1:2], [0:32], [1:4], [0:128]} | slice | bytes 1572864 | tf_op jit(solution)/shard_map/slice | solution.py:29
  3.0 1.0 pad_maximum_fusion.1
  4.0 6.4 %all-to-all-start.1 = ((f32[4,400,128]{2,1,0:T(8,128)}), f32[4,400,128]{2,1,0:T(8,128)S(1)}, u32[]{:S(2)}, u32[]{:S(2)}) async-start(f32[4,400,128]{2,1,0:T(8,128)} %pad_maximum_fusion.1), calls=%async_computation.1 | async-start | bytes 1638400 | tf_op jit(solution)/shard_map/all_to_all | solution.py:12
  10.9 3.1 %collective-permute-start = (f32[1,656,128]{2,1,0:T(8,128)S(1)}, f32[1,656,128]{2,1,0:T(8,128)S(1)}, u32[]{:S(2)}, u32[]{:S(2)}) collective-permute-start(f32[1,656,128]{2,1,0:T(8,128)S(1)} %get-tuple-element.16), channel_id=1, source_target_pairs={{0,32},{32,64},{64,96},{96,0},{1,33},{33,65},{65,97},{97,1},{2,34}... | collective-permute-start | bytes 1007624 | tf_op jit(solution)/shard_map/ppermute | solution.py:41
  14.1 3.4 %collective-permute-start.1 = (f32[1,656,128]{2,1,0:T(8,128)S(1)}, f32[1,656,128]{2,1,0:T(8,128)S(1)}, u32[]{:S(2)}, u32[]{:S(2)}) collective-permute-start(f32[1,656,128]{2,1,0:T(8,128)S(1)} %get-tuple-element.17), channel_id=1, source_target_pairs={{0,96},{32,0},{64,32},{96,64},{1,97},{33,1},{65,33},{97,65},{2,98}... | collective-permute-start | bytes 1007624 | tf_op jit(solution)/shard_map/ppermute | solution.py:41
  17.5 3.4 %collective-permute-start.2 = (f32[1,656,128]{2,1,0:T(8,128)S(1)}, f32[1,656,128]{2,1,0:T(8,128)S(1)}, u32[]{:S(2)}, u32[]{:S(2)}) collective-permute-start(f32[1,656,128]{2,1,0:T(8,128)S(1)} %get-tuple-element.14), channel_id=1, source_target_pairs={{0,64},{32,96},{64,0},{96,32},{1,65},{33,97},{65,1},{97,33},{2,66}... | collective-permute-start | bytes 1007624 | tf_op jit(solution)/shard_map/ppermute | solution.py:41
  20.9 1.6 %collective-permute-done.1 = f32[1,656,128]{2,1,0:T(8,128)S(1)} collective-permute-done((f32[1,656,128]{2,1,0:T(8,128)S(1)}, f32[1,656,128]{2,1,0:T(8,128)S(1)}, u32[]{:S(2)}, u32[]{:S(2)}) %collective-permute-start.1) | collective-permute-done | bytes 335904 | tf_op jit(solution)/shard_map/ppermute | solution.py:41
  22.7 0.9 convolution_bitcast_fusion
  23.6 4.7 %collective-permute-done.2 = f32[1,656,128]{2,1,0:T(8,128)S(1)} collective-permute-done((f32[1,656,128]{2,1,0:T(8,128)S(1)}, f32[1,656,128]{2,1,0:T(8,128)S(1)}, u32[]{:S(2)}, u32[]{:S(2)}) %collective-permute-start.2) | collective-permute-done | bytes 335904 | tf_op jit(solution)/shard_map/ppermute | solution.py:41
  28.3 0.7 convolution_bitcast_fusion.1
  29.1 0.9 add.70
  30.0 4.6 %all-to-all-start = ((f32[4,5,64,128]{3,2,1,0:T(8,128)}), f32[4,5,64,128]{3,2,1,0:T(8,128)S(1)}, u32[]{:S(2)}, u32[]{:S(2)}) async-start(f32[4,5,64,128]{3,2,1,0:T(8,128)} %bitcast.17), calls=%async_computation | async-start | bytes 1310720 | tf_op jit(solution)/shard_map/all_to_all | solution.py:12
  35.4 5.1 %collective-permute-start.3 = (f32[1,3,64,128]{3,2,1,0:T(8,128)S(1)}, f32[1,3,64,128]{3,2,1,0:T(8,128)S(1)}, u32[]{:S(2)}, u32[]{:S(2)}) collective-permute-start(f32[1,3,64,128]{3,2,1,0:T(8,128)S(1)} %get-tuple-element.20), channel_id=1, source_target_pairs={{0,32},{32,64},{64,96},{96,0},{1,33},{33,65},{65,97},{97,1},{2,34}... | collective-permute-start | bytes 294920 | tf_op jit(solution)/shard_map/ppermute | solution.py:55
  40.4 3.7 %collective-permute-start.5 = (f32[1,3,64,128]{3,2,1,0:T(8,128)S(1)}, f32[1,3,64,128]{3,2,1,0:T(8,128)S(1)}, u32[]{:S(2)}, u32[]{:S(2)}) collective-permute-start(f32[1,3,64,128]{3,2,1,0:T(8,128)S(1)} %get-tuple-element.21), channel_id=1, source_target_pairs={{0,64},{32,96},{64,0},{96,32},{1,65},{33,97},{65,1},{97,33},{2,66}... | collective-permute-start | bytes 294920 | tf_op jit(solution)/shard_map/ppermute | solution.py:55
  44.1 2.6 %collective-permute-start.4 = (f32[1,3,64,128]{3,2,1,0:T(8,128)S(1)}, f32[1,3,64,128]{3,2,1,0:T(8,128)S(1)}, u32[]{:S(2)}, u32[]{:S(2)}) collective-permute-start(f32[1,3,64,128]{3,2,1,0:T(8,128)S(1)} %get-tuple-element.22), channel_id=1, source_target_pairs={{0,96},{32,0},{64,32},{96,64},{1,97},{33,1},{65,33},{97,65},{2,98}... | collective-permute-start | bytes 294920 | tf_op jit(solution)/shard_map/ppermute | solution.py:55
  47.5 2.3 %collective-permute-done.4 = f32[1,3,64,128]{3,2,1,0:T(8,128)S(1)} collective-permute-done((f32[1,3,64,128]{3,2,1,0:T(8,128)S(1)}, f32[1,3,64,128]{3,2,1,0:T(8,128)S(1)}, u32[]{:S(2)}, u32[]{:S(2)}) %collective-permute-start.4) | collective-permute-done | bytes 98336 | tf_op jit(solution)/shard_map/ppermute | solution.py:55
  50.1 17.6 %all_to_all.30 = f32[4,512,128]{1,2,0:T(8,128)S(1)} all-to-all(f32[4,512,128]{1,2,0:T(8,128)S(1)} %broadcast_in_dim.9), channel_id=1, replica_groups=mesh['zm'=2,'zn'=2,'x'=4,'y'=4,'zh'=4,'c'=2] {'y'}, dimensions={0} | all-to-all | bytes 2097152 | tf_op jit(solution)/shard_map/all_to_all | solution.py:12
  67.7 0.7 fusion
  68.5 16.8 %all_to_all.31 = f32[16,8,512]{2,1,0:T(8,128)S(1)} all-to-all(f32[16,8,512]{2,1,0:T(8,128)S(1)} %fusion), channel_id=1, replica_groups=mesh['zm'=2,'zn'=2,'x'=4,'y'=4,'zh'=4,'c'=2] {'zn','x','c'}, dimensions={0} | all-to-all | bytes 524288 | tf_op jit(solution)/shard_map/all_to_all | solution.py:12
  85.3 24.6 %all_to_all.32 = f32[8,8,512]{2,1,0:T(8,128)S(1)} all-to-all(f32[8,8,512]{2,1,0:T(8,128)S(1)} %broadcast_in_dim.10), channel_id=1, replica_groups=mesh['zm'=2,'zn'=2,'x'=4,'y'=4,'zh'=4,'c'=2] {'zm','zh'}, dimensions={0} | all-to-all | bytes 262144 | tf_op jit(solution)/shard_map/all_to_all | solution.py:12
  109.9 0.7 broadcast_in_dim.11
  110.6 7.8 %all-to-all-start.5 = ((f32[16,8,512]{2,1,0:T(8,128)}), f32[16,8,512]{2,1,0:T(8,128)S(1)}, u32[]{:S(2)}, u32[]{:S(2)}) async-start(f32[16,8,512]{2,1,0:T(8,128)} %broadcast_in_dim.11), calls=%async_computation.5 | async-start | bytes 524288 | tf_op jit(solution)/shard_map/all_to_all | solution.py:12
  118.4 0.9 copy.17
  119.3 6.3 %all-to-all-done.5 = f32[16,8,512]{2,1,0:T(8,128)S(1)} async-done(((f32[16,8,512]{2,1,0:T(8,128)}), f32[16,8,512]{2,1,0:T(8,128)S(1)}, u32[]{:S(2)}, u32[]{:S(2)}) %all-to-all-start.5) | async-done | bytes 262176 | tf_op jit(solution)/shard_map/all_to_all | solution.py:12
  (31 shorter events, 4.1 us)
Async XLA Ops:
  3.0 7.4 %copy-start = (f32[32,32,4,128]{3,2,1,0:T(4,128)S(1)}, f32[32,32,4,128]{3,2,1,0:T(4,128)}, u32[]{:S(2)}) copy-start(f32[32,32,4,128]{3,2,1,0:T(4,128)} %param.2) | copy-start | bytes 6291460
  4.0 26.0 %all-to-all-start.1 = ((f32[4,400,128]{2,1,0:T(8,128)}), f32[4,400,128]{2,1,0:T(8,128)S(1)}, u32[]{:S(2)}, u32[]{:S(2)}) async-start(f32[4,400,128]{2,1,0:T(8,128)} %pad_maximum_fusion.1), calls=%async_computation.1 | async-start | bytes 1638400 | tf_op jit(solution)/shard_map/all_to_all | solution.py:12
  10.9 10.0 %collective-permute-start = (f32[1,656,128]{2,1,0:T(8,128)S(1)}, f32[1,656,128]{2,1,0:T(8,128)S(1)}, u32[]{:S(2)}, u32[]{:S(2)}) collective-permute-start(f32[1,656,128]{2,1,0:T(8,128)S(1)} %get-tuple-element.16), channel_id=1, source_target_pairs={{0,32},{32,64},{64,96},{96,0},{1,33},{33,65},{65,97},{97,1},{2,34}... | collective-permute-start | bytes 1007624 | tf_op jit(solution)/shard_map/ppermute | solution.py:41
  14.1 8.5 %collective-permute-start.1 = (f32[1,656,128]{2,1,0:T(8,128)S(1)}, f32[1,656,128]{2,1,0:T(8,128)S(1)}, u32[]{:S(2)}, u32[]{:S(2)}) collective-permute-start(f32[1,656,128]{2,1,0:T(8,128)S(1)} %get-tuple-element.17), channel_id=1, source_target_pairs={{0,96},{32,0},{64,32},{96,64},{1,97},{33,1},{65,33},{97,65},{2,98}... | collective-permute-start | bytes 1007624 | tf_op jit(solution)/shard_map/ppermute | solution.py:41
  17.5 10.8 %collective-permute-start.2 = (f32[1,656,128]{2,1,0:T(8,128)S(1)}, f32[1,656,128]{2,1,0:T(8,128)S(1)}, u32[]{:S(2)}, u32[]{:S(2)}) collective-permute-start(f32[1,656,128]{2,1,0:T(8,128)S(1)} %get-tuple-element.14), channel_id=1, source_target_pairs={{0,64},{32,96},{64,0},{96,32},{1,65},{33,97},{65,1},{97,33},{2,66}... | collective-permute-start | bytes 1007624 | tf_op jit(solution)/shard_map/ppermute | solution.py:41
  30.0 16.7 %all-to-all-start = ((f32[4,5,64,128]{3,2,1,0:T(8,128)}), f32[4,5,64,128]{3,2,1,0:T(8,128)S(1)}, u32[]{:S(2)}, u32[]{:S(2)}) async-start(f32[4,5,64,128]{3,2,1,0:T(8,128)} %bitcast.17), calls=%async_computation | async-start | bytes 1310720 | tf_op jit(solution)/shard_map/all_to_all | solution.py:12
  35.4 11.4 %collective-permute-start.3 = (f32[1,3,64,128]{3,2,1,0:T(8,128)S(1)}, f32[1,3,64,128]{3,2,1,0:T(8,128)S(1)}, u32[]{:S(2)}, u32[]{:S(2)}) collective-permute-start(f32[1,3,64,128]{3,2,1,0:T(8,128)S(1)} %get-tuple-element.20), channel_id=1, source_target_pairs={{0,32},{32,64},{64,96},{96,0},{1,33},{33,65},{65,97},{97,1},{2,34}... | collective-permute-start | bytes 294920 | tf_op jit(solution)/shard_map/ppermute | solution.py:55
  40.4 7.0 %collective-permute-start.5 = (f32[1,3,64,128]{3,2,1,0:T(8,128)S(1)}, f32[1,3,64,128]{3,2,1,0:T(8,128)S(1)}, u32[]{:S(2)}, u32[]{:S(2)}) collective-permute-start(f32[1,3,64,128]{3,2,1,0:T(8,128)S(1)} %get-tuple-element.21), channel_id=1, source_target_pairs={{0,64},{32,96},{64,0},{96,32},{1,65},{33,97},{65,1},{97,33},{2,66}... | collective-permute-start | bytes 294920 | tf_op jit(solution)/shard_map/ppermute | solution.py:55
  44.1 5.7 %collective-permute-start.4 = (f32[1,3,64,128]{3,2,1,0:T(8,128)S(1)}, f32[1,3,64,128]{3,2,1,0:T(8,128)S(1)}, u32[]{:S(2)}, u32[]{:S(2)}) collective-permute-start(f32[1,3,64,128]{3,2,1,0:T(8,128)S(1)} %get-tuple-element.22), channel_id=1, source_target_pairs={{0,96},{32,0},{64,32},{96,64},{1,97},{33,1},{65,33},{97,65},{2,98}... | collective-permute-start | bytes 294920 | tf_op jit(solution)/shard_map/ppermute | solution.py:55
  110.6 14.9 %all-to-all-start.5 = ((f32[16,8,512]{2,1,0:T(8,128)}), f32[16,8,512]{2,1,0:T(8,128)S(1)}, u32[]{:S(2)}, u32[]{:S(2)}) async-start(f32[16,8,512]{2,1,0:T(8,128)} %broadcast_in_dim.11), calls=%async_computation.5 | async-start | bytes 524288 | tf_op jit(solution)/shard_map/all_to_all | solution.py:12

commit v8 on v7

--- a/solution.py
+++ b/solution.py
@@ -45,9 +45,9 @@
         rows_of = jnp.concatenate([got[:, -i // 2 :, :r], got[:, -i // 2 :, r:]], axis=1)
         return jnp.einsum("xir,xuij->urj", rows_of, field, precision=HIGHEST)
 
-    products, last = lax.optimization_barrier((product(jnp.concatenate(got[:-1])), got[-1]))
+    products, other, last = lax.optimization_barrier((product(jnp.concatenate(got[:-1])), product(came), got[-1]))
+    other = other.reshape(nx, -1, r, j)
     products = (products + product(last)).reshape(nzl, -1, r, j)
-    other = product(came).reshape(nx, -1, r, j)
 
     sums = exchange(products, ZL).sum(axis=0)
     tail = pick(other, me_x)[0]

time: 127 us -> 127 us (level)
    all_to_all x3, waiting for transfers between devices: 6.3 us -> 12.3 us  [exchange(): return lax.all_to_all(a, axes, 0, 0)]
    ppermute x3, waiting for transfers between devices: 6.31 us -> 1.64 us  [local(): lax.ppermute(pick(rest, (me_x + d) % nx), 'x', [(x, (x + d) % nx) for x i...]
  transfers between devices with their start and end apart: 9 -> 9, of which waited for: 5 -> 4; matrix products, arithmetic and copies ran while one was open for 4% -> 2% of each run, Pallas kernels for 0% -> 0%
where the time goes in v8:
time: 127 us; the launch traced here: 126 us
  blocking collectives  58.9 us (46%)
  starting transfers between devices  39.3 us (31%)
  waiting for transfers between devices  16.5 us (13%)
  local copies, waits for them, and re-layouts  5.56 us (4%)
  matrix products  2.9 us (2%)
  other arithmetic  2.25 us (2%)
    all_to_all x3, blocking collectives, exchange(): return lax.all_to_all(a, axes, 0, 0)  58.9 us
    all_to_all x3, starting transfers between devices, exchange(): return lax.all_to_all(a, axes, 0, 0)  17.7 us
    all_to_all x3, waiting for transfers between devices, exchange(): return lax.all_to_all(a, axes, 0, 0)  12.3 us
    ppermute x3, starting transfers between devices, local(): lax.ppermute(pick(other, (me_x + d) % nx), 'x', [(x, (x + d) % nx) for x...  11.7 us
    ppermute x3, starting transfers between devices, local(): lax.ppermute(pick(rest, (me_x + d) % nx), 'x', [(x, (x + d) % nx) for x i...  9.93 us
    ppermute x3, waiting for transfers between devices, local(): lax.ppermute(pick(other, (me_x + d) % nx), 'x', [(x, (x + d) % nx) for x...  2.57 us
  transfers between devices with their start and end apart: 9, of which 4 were waited for; matrix products, arithmetic and copies ran while one was open for 2% of the time, Pallas kernels for 0%

profile of v8, /device:TPU:1, one launch (start us, length us, event | category | flops | bytes accessed | tf_op | source)
XLA Modules:
  0.0 126.3 jit_solution(12253966306321002427)
XLA Ops:
  1.3 1.5 %slice.52 = f32[4,4,1,32,3,128]{5,4,3,2,1,0:T(4,128)S(1)} slice(f32[4,4,2,32,4,128]{5,4,3,2,1,0:T(4,128)} %bitcast.62), slice={[0:4], [0:4], [1:2], [0:32], [1:4], [0:128]} | slice | bytes 1572864 | tf_op jit(solution)/shard_map/slice | solution.py:29
  3.0 1.0 pad_maximum_fusion.1
  4.0 6.4 %all-to-all-start = ((f32[4,400,128]{2,1,0:T(8,128)}), f32[4,400,128]{2,1,0:T(8,128)S(1)}, u32[]{:S(2)}, u32[]{:S(2)}) async-start(f32[4,400,128]{2,1,0:T(8,128)} %pad_maximum_fusion.1), calls=%async_computation | async-start | bytes 1638400 | tf_op jit(solution)/shard_map/all_to_all | solution.py:12
  10.9 3.1 %collective-permute-start = (f32[1,656,128]{2,1,0:T(8,128)S(1)}, f32[1,656,128]{2,1,0:T(8,128)S(1)}, u32[]{:S(2)}, u32[]{:S(2)}) collective-permute-start(f32[1,656,128]{2,1,0:T(8,128)S(1)} %get-tuple-element.18), channel_id=1, source_target_pairs={{0,32},{32,64},{64,96},{96,0},{1,33},{33,65},{65,97},{97,1},{2,34}... | collective-permute-start | bytes 1007624 | tf_op jit(solution)/shard_map/ppermute | solution.py:41
  14.1 3.4 %collective-permute-start.1 = (f32[1,656,128]{2,1,0:T(8,128)S(1)}, f32[1,656,128]{2,1,0:T(8,128)S(1)}, u32[]{:S(2)}, u32[]{:S(2)}) collective-permute-start(f32[1,656,128]{2,1,0:T(8,128)S(1)} %get-tuple-element.19), channel_id=1, source_target_pairs={{0,96},{32,0},{64,32},{96,64},{1,97},{33,1},{65,33},{97,65},{2,98}... | collective-permute-start | bytes 1007624 | tf_op jit(solution)/shard_map/ppermute | solution.py:41
  17.5 3.4 %collective-permute-start.2 = (f32[1,656,128]{2,1,0:T(8,128)S(1)}, f32[1,656,128]{2,1,0:T(8,128)S(1)}, u32[]{:S(2)}, u32[]{:S(2)}) collective-permute-start(f32[1,656,128]{2,1,0:T(8,128)S(1)} %get-tuple-element.16), channel_id=1, source_target_pairs={{0,64},{32,96},{64,0},{96,32},{1,65},{33,97},{65,1},{97,33},{2,66}... | collective-permute-start | bytes 1007624 | tf_op jit(solution)/shard_map/ppermute | solution.py:41
  20.9 1.6 %collective-permute-done.1 = f32[1,656,128]{2,1,0:T(8,128)S(1)} collective-permute-done((f32[1,656,128]{2,1,0:T(8,128)S(1)}, f32[1,656,128]{2,1,0:T(8,128)S(1)}, u32[]{:S(2)}, u32[]{:S(2)}) %collective-permute-start.1) | collective-permute-done | bytes 335904 | tf_op jit(solution)/shard_map/ppermute | solution.py:41
  22.7 0.9 convolution_bitcast_fusion
  23.6 6.0 %all-to-all-done = f32[4,400,128]{2,1,0:T(8,128)S(1)} async-done(((f32[4,400,128]{2,1,0:T(8,128)}), f32[4,400,128]{2,1,0:T(8,128)S(1)}, u32[]{:S(2)}, u32[]{:S(2)}) %all-to-all-start) | async-done | bytes 819232 | tf_op jit(solution)/shard_map/all_to_all | solution.py:12
  30.4 0.7 convolution_bitcast_fusion.1
  31.1 0.9 add.70
  32.1 3.5 %all-to-all-start.1 = ((f32[4,5,64,128]{3,2,1,0:T(8,128)}), f32[4,5,64,128]{3,2,1,0:T(8,128)S(1)}, u32[]{:S(2)}, u32[]{:S(2)}) async-start(f32[4,5,64,128]{3,2,1,0:T(8,128)} %bitcast.23), calls=%async_computation.1 | async-start | bytes 1310720 | tf_op jit(solution)/shard_map/all_to_all | solution.py:12
  35.6 4.3 %collective-permute-start.3 = (f32[1,3,64,128]{3,2,1,0:T(8,128)S(1)}, f32[1,3,64,128]{3,2,1,0:T(8,128)S(1)}, u32[]{:S(2)}, u32[]{:S(2)}) collective-permute-start(f32[1,3,64,128]{3,2,1,0:T(8,128)S(1)} %get-tuple-element.22), channel_id=1, source_target_pairs={{0,32},{32,64},{64,96},{96,0},{1,33},{33,65},{65,97},{97,1},{2,34}... | collective-permute-start | bytes 294920 | tf_op jit(solution)/shard_map/ppermute | solution.py:55
  39.9 4.3 %collective-permute-start.5 = (f32[1,3,64,128]{3,2,1,0:T(8,128)S(1)}, f32[1,3,64,128]{3,2,1,0:T(8,128)S(1)}, u32[]{:S(2)}, u32[]{:S(2)}) collective-permute-start(f32[1,3,64,128]{3,2,1,0:T(8,128)S(1)} %get-tuple-element.23), channel_id=1, source_target_pairs={{0,64},{32,96},{64,0},{96,32},{1,65},{33,97},{65,1},{97,33},{2,66}... | collective-permute-start | bytes 294920 | tf_op jit(solution)/shard_map/ppermute | solution.py:55
  44.2 3.1 %collective-permute-start.4 = (f32[1,3,64,128]{3,2,1,0:T(8,128)S(1)}, f32[1,3,64,128]{3,2,1,0:T(8,128)S(1)}, u32[]{:S(2)}, u32[]{:S(2)}) collective-permute-start(f32[1,3,64,128]{3,2,1,0:T(8,128)S(1)} %get-tuple-element.24), channel_id=1, source_target_pairs={{0,96},{32,0},{64,32},{96,64},{1,97},{33,1},{65,33},{97,65},{2,98}... | collective-permute-start | bytes 294920 | tf_op jit(solution)/shard_map/ppermute | solution.py:55
  47.3 2.6 %collective-permute-done.4 = f32[1,3,64,128]{3,2,1,0:T(8,128)S(1)} collective-permute-done((f32[1,3,64,128]{3,2,1,0:T(8,128)S(1)}, f32[1,3,64,128]{3,2,1,0:T(8,128)S(1)}, u32[]{:S(2)}, u32[]{:S(2)}) %collective-permute-start.4) | collective-permute-done | bytes 98336 | tf_op jit(solution)/shard_map/ppermute | solution.py:55
  50.3 14.0 %all_to_all.30 = f32[4,512,128]{1,2,0:T(8,128)S(1)} all-to-all(f32[4,512,128]{1,2,0:T(8,128)S(1)} %broadcast_in_dim.9), channel_id=1, replica_groups=mesh['zm'=2,'zn'=2,'x'=4,'y'=4,'zh'=4,'c'=2] {'y'}, dimensions={0} | all-to-all | bytes 2097152 | tf_op jit(solution)/shard_map/all_to_all | solution.py:12
  64.2 0.7 fusion
  65.0 20.9 %all_to_all.31 = f32[16,8,512]{2,1,0:T(8,128)S(1)} all-to-all(f32[16,8,512]{2,1,0:T(8,128)S(1)} %fusion), channel_id=1, replica_groups=mesh['zm'=2,'zn'=2,'x'=4,'y'=4,'zh'=4,'c'=2] {'zn','x','c'}, dimensions={0} | all-to-all | bytes 524288 | tf_op jit(solution)/shard_map/all_to_all | solution.py:12
  85.9 24.1 %all_to_all.32 = f32[8,8,512]{2,1,0:T(8,128)S(1)} all-to-all(f32[8,8,512]{2,1,0:T(8,128)S(1)} %broadcast_in_dim.10), channel_id=1, replica_groups=mesh['zm'=2,'zn'=2,'x'=4,'y'=4,'zh'=4,'c'=2] {'zm','zh'}, dimensions={0} | all-to-all | bytes 262144 | tf_op jit(solution)/shard_map/all_to_all | solution.py:12
  110.0 0.7 broadcast_in_dim.11
  110.7 7.8 %all-to-all-start.5 = ((f32[16,8,512]{2,1,0:T(8,128)}), f32[16,8,512]{2,1,0:T(8,128)S(1)}, u32[]{:S(2)}, u32[]{:S(2)}) async-start(f32[16,8,512]{2,1,0:T(8,128)} %broadcast_in_dim.11), calls=%async_computation.5 | async-start | bytes 524288 | tf_op jit(solution)/shard_map/all_to_all | solution.py:12
  118.5 0.9 copy.17
  119.3 6.3 %all-to-all-done.5 = f32[16,8,512]{2,1,0:T(8,128)S(1)} async-done(((f32[16,8,512]{2,1,0:T(8,128)}), f32[16,8,512]{2,1,0:T(8,128)S(1)}, u32[]{:S(2)}, u32[]{:S(2)}) %all-to-all-start.5) | async-done | bytes 262176 | tf_op jit(solution)/shard_map/all_to_all | solution.py:12
  (31 shorter events, 3.5 us)
Async XLA Ops:
  3.0 7.4 %copy-start = (f32[32,32,4,128]{3,2,1,0:T(4,128)S(1)}, f32[32,32,4,128]{3,2,1,0:T(4,128)}, u32[]{:S(2)}) copy-start(f32[32,32,4,128]{3,2,1,0:T(4,128)} %param.2) | copy-start | bytes 6291460
  4.0 25.6 %all-to-all-start = ((f32[4,400,128]{2,1,0:T(8,128)}), f32[4,400,128]{2,1,0:T(8,128)S(1)}, u32[]{:S(2)}, u32[]{:S(2)}) async-start(f32[4,400,128]{2,1,0:T(8,128)} %pad_maximum_fusion.1), calls=%async_computation | async-start | bytes 1638400 | tf_op jit(solution)/shard_map/all_to_all | solution.py:12
  10.9 10.0 %collective-permute-start = (f32[1,656,128]{2,1,0:T(8,128)S(1)}, f32[1,656,128]{2,1,0:T(8,128)S(1)}, u32[]{:S(2)}, u32[]{:S(2)}) collective-permute-start(f32[1,656,128]{2,1,0:T(8,128)S(1)} %get-tuple-element.18), channel_id=1, source_target_pairs={{0,32},{32,64},{64,96},{96,0},{1,33},{33,65},{65,97},{97,1},{2,34}... | collective-permute-start | bytes 1007624 | tf_op jit(solution)/shard_map/ppermute | solution.py:41
  14.1 8.5 %collective-permute-start.1 = (f32[1,656,128]{2,1,0:T(8,128)S(1)}, f32[1,656,128]{2,1,0:T(8,128)S(1)}, u32[]{:S(2)}, u32[]{:S(2)}) collective-permute-start(f32[1,656,128]{2,1,0:T(8,128)S(1)} %get-tuple-element.19), channel_id=1, source_target_pairs={{0,96},{32,0},{64,32},{96,64},{1,97},{33,1},{65,33},{97,65},{2,98}... | collective-permute-start | bytes 1007624 | tf_op jit(solution)/shard_map/ppermute | solution.py:41
  17.5 12.8 %collective-permute-start.2 = (f32[1,656,128]{2,1,0:T(8,128)S(1)}, f32[1,656,128]{2,1,0:T(8,128)S(1)}, u32[]{:S(2)}, u32[]{:S(2)}) collective-permute-start(f32[1,656,128]{2,1,0:T(8,128)S(1)} %get-tuple-element.16), channel_id=1, source_target_pairs={{0,64},{32,96},{64,0},{96,32},{1,65},{33,97},{65,1},{97,33},{2,66}... | collective-permute-start | bytes 1007624 | tf_op jit(solution)/shard_map/ppermute | solution.py:41
  32.1 17.9 %all-to-all-start.1 = ((f32[4,5,64,128]{3,2,1,0:T(8,128)}), f32[4,5,64,128]{3,2,1,0:T(8,128)S(1)}, u32[]{:S(2)}, u32[]{:S(2)}) async-start(f32[4,5,64,128]{3,2,1,0:T(8,128)} %bitcast.23), calls=%async_computation.1 | async-start | bytes 1310720 | tf_op jit(solution)/shard_map/all_to_all | solution.py:12
  35.6 11.7 %collective-permute-start.3 = (f32[1,3,64,128]{3,2,1,0:T(8,128)S(1)}, f32[1,3,64,128]{3,2,1,0:T(8,128)S(1)}, u32[]{:S(2)}, u32[]{:S(2)}) collective-permute-start(f32[1,3,64,128]{3,2,1,0:T(8,128)S(1)} %get-tuple-element.22), channel_id=1, source_target_pairs={{0,32},{32,64},{64,96},{96,0},{1,33},{33,65},{65,97},{97,1},{2,34}... | collective-permute-start | bytes 294920 | tf_op jit(solution)/shard_map/ppermute | solution.py:55
  39.9 7.4 %collective-permute-start.5 = (f32[1,3,64,128]{3,2,1,0:T(8,128)S(1)}, f32[1,3,64,128]{3,2,1,0:T(8,128)S(1)}, u32[]{:S(2)}, u32[]{:S(2)}) collective-permute-start(f32[1,3,64,128]{3,2,1,0:T(8,128)S(1)} %get-tuple-element.23), channel_id=1, source_target_pairs={{0,64},{32,96},{64,0},{96,32},{1,65},{33,97},{65,1},{97,33},{2,66}... | collective-permute-start | bytes 294920 | tf_op jit(solution)/shard_map/ppermute | solution.py:55
  44.2 5.7 %collective-permute-start.4 = (f32[1,3,64,128]{3,2,1,0:T(8,128)S(1)}, f32[1,3,64,128]{3,2,1,0:T(8,128)S(1)}, u32[]{:S(2)}, u32[]{:S(2)}) collective-permute-start(f32[1,3,64,128]{3,2,1,0:T(8,128)S(1)} %get-tuple-element.24), channel_id=1, source_target_pairs={{0,96},{32,0},{64,32},{96,64},{1,97},{33,1},{65,33},{97,65},{2,98}... | collective-permute-start | bytes 294920 | tf_op jit(solution)/shard_map/ppermute | solution.py:55
  110.7 14.9 %all-to-all-start.5 = ((f32[16,8,512]{2,1,0:T(8,128)}), f32[16,8,512]{2,1,0:T(8,128)S(1)}, u32[]{:S(2)}, u32[]{:S(2)}) async-start(f32[16,8,512]{2,1,0:T(8,128)} %broadcast_in_dim.11), calls=%async_computation.5 | async-start | bytes 524288 | tf_op jit(solution)/shard_map/all_to_all | solution.py:12
